TPU v7x, 256 devices: a whole 4x4x8 slice. The times are simulated.
256 devices in a mesh: section: 4 (over z_hi), fsdp: 64 (over z_lo, y, x, core).
Axes of the slice: x: 4, y: 4, z: 8 (z_hi: 4, z_lo: 2; z = z_hi * 2 + z_lo), core: 2. Of those that a mesh axis runs over, the one named last changes fastest.
Arguments:
- inputs: bfloat16 [2, 8192, 2048], P(None, 'fsdp'), may hold values from -6 to 6
- weights: bfloat16 [4, 2048, 2048], P('section', 'fsdp'), may hold values from -0.125 to 0.125
- cotangents: bfloat16 [2, 8192, 2048], P(None, 'fsdp'), may hold values from -0.125 to 0.125
- lengths: int32 [2, 128], P(None, 'fsdp'), may hold values from 1 to 64
Outputs:
- weight_grads: float32 [4, 2048, 2048], P('section', 'fsdp')
Inputs may be any that keep to these rules, and one draw needn't show every extreme that they name: `lengths`: each sequence's count of real tokens; its other positions up to 64 are padding.
All inputs are finite; a program needn't handle non-finite values.
Results may differ from a plain program's by a relative error of at most 0.009.
Values may be sent and summed in bfloat16 or wider, within the bound.
A program may use at most 128 MiB of HBM per device.

v0:
```python
import jax
import jax.numpy as jnp
from jax import lax
from jax.sharding import PartitionSpec as P

epsilon = 1e-06


def shifted(block, axis, distance):
    devices = range(lax.axis_size(axis))
    route = [(i - distance, i) for i in devices if i - distance in devices]
    return lax.ppermute(block, axis, route)


def section_forward(section_input, section_weight):
    as_float = section_input.astype(jnp.float32)
    inverse = lax.rsqrt(jnp.mean(as_float * as_float, axis=-1, keepdims=True) + epsilon)
    normed = (as_float * inverse).astype(jnp.bfloat16)
    preact = jnp.dot(normed, section_weight, preferred_element_type=jnp.float32)
    return (as_float, inverse, normed, preact)


def forward_keep(section_input, section_weight):
    as_float, inverse, normed, preact = section_forward(section_input, section_weight)
    return ((as_float + jax.nn.gelu(preact)).astype(jnp.bfloat16), inverse, normed, preact)


def spare_forward(section_input, section_weight):
    row_count = section_input.shape[0]
    inverse = jnp.zeros((row_count, 1), jnp.float32)
    preact = jnp.zeros((row_count, section_weight.shape[1]), jnp.float32)
    return (section_input, inverse, jnp.zeros_like(section_input), preact)


def kept_backward(section_input, inverse, normed, preact, section_weight, grad_output):
    as_float = section_input.astype(jnp.float32)
    grad_float = grad_output.astype(jnp.float32)
    unused, pullback = jax.vjp(jax.nn.gelu, preact)
    grad_pre = pullback(grad_float)[0].astype(jnp.bfloat16)
    grad_normed = lax.dot_general(
        grad_pre, section_weight, (((1,), (1,)), ((), ())), preferred_element_type=jnp.float32
    )
    grad_input = (
        grad_float
        + inverse * grad_normed
        - as_float * inverse**3 * jnp.mean(grad_normed * as_float, axis=-1, keepdims=True)
    )
    return (grad_input.astype(jnp.bfloat16), normed, grad_pre)


def spare_backward(section_input, inverse, normed, preact, section_weight, grad_output):
    blank_rows = jnp.zeros_like(section_input)
    return (grad_output, blank_rows, blank_rows)


def toward_last(values):
    return shifted(values, "section", 1)


def toward_first(values):
    return shifted(values, "section", -1)


def gradient_share(normed, grad_pre):
    return lax.psum_scatter(
        lax.dot_general(
            normed, grad_pre, (((0,), (0,)), ((), ())), preferred_element_type=jnp.float32
        ),
        "fsdp",
        scatter_dimension=0,
        tiled=True,
    )


def keep_where(active, fresh, kept):
    return tuple(
        (jnp.where(active, new_value, old_value) for new_value, old_value in zip(fresh, kept))
    )


def blank_state(rows, features):
    return (
        jnp.zeros((rows, features), jnp.bfloat16),
        jnp.zeros((rows, 1), jnp.float32),
        jnp.zeros((rows, features), jnp.bfloat16),
        jnp.zeros((rows, features), jnp.float32),
    )


def local(inputs, weights, cotangents, lengths):
    sections = lax.axis_size("section")
    section_index = lax.axis_index("section")
    tok_rows = inputs.shape[1]
    features = inputs.shape[2]
    seq_length = tok_rows // lengths.shape[1]
    positions = jnp.arange(seq_length, dtype=jnp.int32)
    live_rows = (positions[None, None, :] < lengths[:, :, None]).reshape(2, tok_rows, 1)
    cot_rows = jnp.where(live_rows, cotangents, jnp.zeros((), cotangents.dtype))
    gathered = lax.all_gather(weights[0], "fsdp", axis=0, tiled=True)
    travelling = jnp.where(
        section_index == 0, inputs.reshape(2 * tok_rows, features), jnp.zeros((), inputs.dtype)
    )
    kept = blank_state(2 * tok_rows, features)
    for tick_index in range(sections):
        active = section_index == tick_index
        result, inverse, normed, preact = lax.cond(
            active, forward_keep, spare_forward, travelling, gathered
        )
        kept = keep_where(active, (travelling, inverse, normed, preact), kept)
        if tick_index + 1 < sections:
            travelling = toward_last(result)
    flowing = jnp.where(
        section_index == sections - 1,
        cot_rows.reshape(2 * tok_rows, features),
        jnp.zeros((), cot_rows.dtype),
    )
    normed_keep = jnp.zeros_like(kept[0])
    grad_keep = jnp.zeros_like(kept[0])
    for tick_index in reversed(range(sections)):
        active = section_index == tick_index
        flowing, normed, grad_pre = lax.cond(
            active,
            kept_backward,
            spare_backward,
            kept[0],
            kept[1],
            kept[2],
            kept[3],
            gathered,
            flowing,
        )
        normed_keep = jnp.where(active, normed, normed_keep)
        grad_keep = jnp.where(active, grad_pre, grad_keep)
        if tick_index > 0:
            flowing = toward_first(flowing)
    share = gradient_share(normed_keep, grad_keep)
    return share[None]


def solution(mesh):
    in_specs = (
        P(None, "fsdp", None),
        P("section", "fsdp", None),
        P(None, "fsdp", None),
        P(None, "fsdp"),
    )
    out_specs = P("section", "fsdp", None)
    return jax.shard_map(local, mesh=mesh, in_specs=in_specs, out_specs=out_specs, check_vma=False)
```

profile of v0, /device:TPU:1, one launch (start us, length us, event | category | flops | bytes accessed | tf_op | source)
XLA Modules:
  0.0 772.8 jit_solution(16982406794057696383)
XLA Ops:
  6.5 0.0 all-gather.3.cloned.1.call-start
  6.5 0.7 all-gather.3.cloned.1.call-update
  7.3 0.0 reduce-scatter.2.cloned.1.call-start
  7.3 2.3 broadcast_select_fusion
  9.6 117.4 %all-gather.3.cloned.1.call-done = bf16[1,2048,2048]{2,1,0:T(8,128)(2,1)} async-done(((bf16[1,32,2048]{2,1,0:T(8,128)(2,1)}), bf16[1,2048,2048]{2,1,0:T(8,128)(2,1)}) %all-gather.3.cloned.1.call-update) | async-done | bytes 8388624 | tf_op jit(solution)/shard_map/all_gather | solution.py:99
  127.1 12.6 %conditional.8 = (bf16[256,2048]{1,0:T(8,128)(2,1)S(1)}, f32[256,1]{0,1:T(1,128)}, bf16[256,2048]{1,0:T(8,128)(2,1)}, f32[256,2048]{1,0:T(8,128)}) conditional(s32[]{:T(128)} %convert_element_type.91, bf16[256,2048]{1,0:T(8,128)(2,1)} %bitcast.11, (bf16[256,2048]{1,0:T(8,128)(2,1)}, bf16[2048,2048]{1,0:T(8,128)(2,1)}) %tuple.107), branch_computations={%region_0.1_spmd, %region_1.3_spmd} | conditional | flops 2156396800 | bytes 16781344 | solution.py:106
  127.1 1.5 fusion
  128.6 0.6 add_rsqrt_fusion
  129.1 2.5 fusion.1
  131.7 8.0 %fusion.2 = (bf16[256,2048]{1,0:T(8,128)(2,1)S(1)}, f32[256,2048]{1,0:T(8,128)}) fusion(bf16[256,2048]{1,0:T(8,128)(2,1)} %get-tuple-element.69, bf16[256,2048]{1,0:T(8,128)(2,1)} %fusion.1, bf16[2048,2048]{1,0:T(8,128)(2,1)} %get-tuple-element.70), kind=kOutput, calls=%fused_computation.6 | convolution fusion | flops 2153250816 | bytes 13631488 | tf_op jit(solution)/shard_map/cond/branch_1_fun/dot_general | solution.py:19
  139.7 2.3 collective-permute-start
  142.0 21.6 %collective-permute-done = bf16[256,2048]{1,0:T(8,128)(2,1)} collective-permute-done((bf16[256,2048]{1,0:T(8,128)(2,1)S(1)}, bf16[256,2048]{1,0:T(8,128)(2,1)}, u32[]{:S(2)}, u32[]{:S(2)}) %collective-permute-start) | collective-permute-done | bytes 1048608 | tf_op jit(solution)/shard_map/ppermute | solution.py:12
  163.6 4.5 conditional.9
  163.6 1.2 copy.17
  164.8 1.6 broadcast.263
  166.5 1.1 broadcast.262
  167.6 0.5 broadcast.261
  168.1 14.2 %collective-permute-start.1 = (bf16[256,2048]{1,0:T(8,128)(2,1)S(1)}, bf16[256,2048]{1,0:T(8,128)(2,1)}, u32[]{:S(2)}, u32[]{:S(2)}) collective-permute-start(bf16[256,2048]{1,0:T(8,128)(2,1)S(1)} %get-tuple-element.125), channel_id=1, source_target_pairs={{0,64},{64,128},{128,192},{1,65},{65,129},{129,193},{2,66},{66,130... | collective-permute-start | bytes 3145736 | tf_op jit(solution)/shard_map/ppermute | solution.py:12
  182.3 20.7 %collective-permute-done.1 = bf16[256,2048]{1,0:T(8,128)(2,1)} collective-permute-done((bf16[256,2048]{1,0:T(8,128)(2,1)S(1)}, bf16[256,2048]{1,0:T(8,128)(2,1)}, u32[]{:S(2)}, u32[]{:S(2)}) %collective-permute-start.1) | collective-permute-done | bytes 1048608 | tf_op jit(solution)/shard_map/ppermute | solution.py:12
  203.0 4.6 conditional.10
  203.0 1.3 copy.25
  204.3 1.6 broadcast.272
  205.9 1.1 broadcast.271
  207.0 0.6 broadcast.270
  207.6 6.2 collective-permute-start.2
  213.8 0.0 copy-done.8
  213.8 0.1 lt.26
  213.9 0.1 lt.27
  214.0 0.1 lt.24
  214.1 0.0 copy-done.7
  214.1 1.1 select_select_fusion.3
  215.2 18.4 %collective-permute-done.2 = bf16[256,2048]{1,0:T(8,128)(2,1)} collective-permute-done((bf16[256,2048]{1,0:T(8,128)(2,1)S(1)}, bf16[256,2048]{1,0:T(8,128)(2,1)}, u32[]{:S(2)}, u32[]{:S(2)}) %collective-permute-start.2) | collective-permute-done | bytes 1048608 | tf_op jit(solution)/shard_map/ppermute | solution.py:12
  233.6 3.3 conditional.11
  233.6 1.6 broadcast.281
  235.2 1.2 broadcast.280
  236.3 0.6 broadcast.279
  236.9 2.6 select_select_fusion
  239.6 0.0 slice-start.1
  239.6 0.9 broadcast_select_fusion.4
  240.4 3.3 select_select_fusion.1
  243.7 0.0 slice-done
  243.8 0.0 slice-done.1
  243.8 0.0 copy-done
  243.8 1.2 conditional.12
  243.8 0.1 broadcast.284
  243.9 1.1 broadcast.284.clone
  245.0 1.3 collective-permute-start.3
  246.3 49.3 %collective-permute-done.3 = bf16[256,2048]{1,0:T(8,128)(2,1)S(1)} collective-permute-done((bf16[256,2048]{1,0:T(8,128)(2,1)S(1)}, bf16[256,2048]{1,0:T(8,128)(2,1)S(1)}, u32[]{:S(2)}, u32[]{:S(2)}) %collective-permute-start.3) | collective-permute-done | bytes 1048608 | tf_op jit(solution)/shard_map/ppermute | solution.py:12
  295.6 0.0 copy-done.1
  295.6 1.3 conditional.13
  295.6 0.1 broadcast.291
  295.7 1.1 broadcast.291.clone
  296.8 1.3 collective-permute-start.4
  298.1 24.7 %collective-permute-done.4 = bf16[256,2048]{1,0:T(8,128)(2,1)S(1)} collective-permute-done((bf16[256,2048]{1,0:T(8,128)(2,1)S(1)}, bf16[256,2048]{1,0:T(8,128)(2,1)S(1)}, u32[]{:S(2)}, u32[]{:S(2)}) %collective-permute-start.4) | collective-permute-done | bytes 1048608 | tf_op jit(solution)/shard_map/ppermute | solution.py:12
  322.8 1.2 conditional.14
  322.8 0.1 broadcast.298
  322.9 1.1 broadcast.298.clone
  324.0 1.3 collective-permute-start.5
  325.3 102.5 %collective-permute-done.5 = bf16[256,2048]{1,0:T(8,128)(2,1)S(1)} collective-permute-done((bf16[256,2048]{1,0:T(8,128)(2,1)S(1)}, bf16[256,2048]{1,0:T(8,128)(2,1)S(1)}, u32[]{:S(2)}, u32[]{:S(2)}) %collective-permute-start.5) | collective-permute-done | bytes 1048608 | tf_op jit(solution)/shard_map/ppermute | solution.py:12
  427.8 2.4 conditional.15
  427.8 2.4 fusion.76
  430.2 9.7 %fusion.84 = f32[2048,2048]{1,0:T(8,128)} fusion(bf16[256,2048]{1,0:T(8,128)(2,1)} %get-tuple-element.146, bf16[256,2048]{1,0:T(8,128)(2,1)} %get-tuple-element.147, bf16[256,2048]{1,0:T(8,128)(2,1)} %get-tuple-element.148, bf16[256,2048]{1,0:T(8,128)(2,1)} %get-tuple-element.149, bf16[256,2048]{1,0:T(8,128)(2,1)S(1)} %get-tuple-element.142, ...), kind=kOutput, calls=%fused_computation.134 | convolution fusion | flops 2151677952 | bytes 25165828 | tf_op jit(solution)/shard_map/dot_general | solution.py:66
  440.0 0.0 reduce-scatter.2.cloned.1.call-update
  440.0 326.0 %reduce-scatter.2.cloned.1.call-done = f32[32,2048]{1,0:T(8,128)} async-done(((f32[2048,2048]{1,0:T(8,128)}), f32[32,2048]{1,0:T(8,128)}) %reduce-scatter.2.cloned.1.call-update) | async-done | bytes 262160 | tf_op jit(solution)/shard_map/reduce_scatter | solution.py:65
  (12 shorter events, 0.0 us)
Async XLA Ops:
  6.5 120.5 %all-gather.3.cloned.1.call-start = ((), (), s32[]{:S(2)}) async-start(), calls=%async_computation.2 | async-start | bytes 8519680 | tf_op jit(solution)/shard_map/all_gather | solution.py:99
  7.3 758.7 %reduce-scatter.2.cloned.1.call-start = ((), (), s32[]{:S(2)}) async-start(), calls=%async_computation.1 | async-start | bytes 17039360 | tf_op jit(solution)/shard_map/reduce_scatter | solution.py:65
  139.7 23.9 %collective-permute-start = (bf16[256,2048]{1,0:T(8,128)(2,1)S(1)}, bf16[256,2048]{1,0:T(8,128)(2,1)}, u32[]{:S(2)}, u32[]{:S(2)}) collective-permute-start(bf16[256,2048]{1,0:T(8,128)(2,1)S(1)} %get-tuple-element.124), channel_id=1, source_target_pairs={{0,64},{64,128},{128,192},{1,65},{65,129},{129,193},{2,66},{66,130... | collective-permute-start | bytes 3145736 | tf_op jit(solution)/shard_map/ppermute | solution.py:12
  168.1 34.9 %collective-permute-start.1 = (bf16[256,2048]{1,0:T(8,128)(2,1)S(1)}, bf16[256,2048]{1,0:T(8,128)(2,1)}, u32[]{:S(2)}, u32[]{:S(2)}) collective-permute-start(bf16[256,2048]{1,0:T(8,128)(2,1)S(1)} %get-tuple-element.125), channel_id=1, source_target_pairs={{0,64},{64,128},{128,192},{1,65},{65,129},{129,193},{2,66},{66,130... | collective-permute-start | bytes 3145736 | tf_op jit(solution)/shard_map/ppermute | solution.py:12
  203.0 10.8 %copy-start.8 = (s32[2,2]{1,0:T(2,128)S(1)}, s32[2,2]{1,0:T(2,128)}, u32[]{:S(2)}) copy-start(s32[2,2]{1,0:T(2,128)} %param.23) | copy-start | bytes 52
  203.0 11.1 %copy-start.7 = (bf16[2,128,2048]{2,1,0:T(8,128)(2,1)S(1)}, bf16[2,128,2048]{2,1,0:T(8,128)(2,1)}, u32[]{:S(2)}) copy-start(bf16[2,128,2048]{2,1,0:T(8,128)(2,1)} %param.22) | copy-start | bytes 3145732
  207.6 26.0 %collective-permute-start.2 = (bf16[256,2048]{1,0:T(8,128)(2,1)S(1)}, bf16[256,2048]{1,0:T(8,128)(2,1)}, u32[]{:S(2)}, u32[]{:S(2)}) collective-permute-start(bf16[256,2048]{1,0:T(8,128)(2,1)S(1)} %get-tuple-element.126), channel_id=1, source_target_pairs={{0,64},{64,128},{128,192},{1,65},{65,129},{129,193},{2,66},{66,130... | collective-permute-start | bytes 3145736 | tf_op jit(solution)/shard_map/ppermute | solution.py:12
  236.9 6.8 slice-start
  239.6 4.2 slice-start.1
  240.4 3.3 copy-start
  245.0 50.6 %copy-start.1 = (bf16[256,2048]{1,0:T(8,128)(2,1)}, bf16[256,2048]{1,0:T(8,128)(2,1)S(1)}, u32[]{:S(2)}) copy-start(bf16[256,2048]{1,0:T(8,128)(2,1)S(1)} %get-tuple-element.145) | copy-start | bytes 3145732
  245.0 50.6 %collective-permute-start.3 = (bf16[256,2048]{1,0:T(8,128)(2,1)S(1)}, bf16[256,2048]{1,0:T(8,128)(2,1)S(1)}, u32[]{:S(2)}, u32[]{:S(2)}) collective-permute-start(bf16[256,2048]{1,0:T(8,128)(2,1)S(1)} %get-tuple-element.139), channel_id=1, source_target_pairs={{64,0},{128,64},{192,128},{65,1},{129,65},{193,129},{66,2},{130,66... | collective-permute-start | bytes 3145736 | tf_op jit(solution)/shard_map/ppermute | solution.py:12
  296.8 25.9 %copy-start.2 = (bf16[256,2048]{1,0:T(8,128)(2,1)}, bf16[256,2048]{1,0:T(8,128)(2,1)S(1)}, u32[]{:S(2)}) copy-start(bf16[256,2048]{1,0:T(8,128)(2,1)S(1)} %get-tuple-element.144) | copy-start | bytes 3145732
  296.8 25.9 %collective-permute-start.4 = (bf16[256,2048]{1,0:T(8,128)(2,1)S(1)}, bf16[256,2048]{1,0:T(8,128)(2,1)S(1)}, u32[]{:S(2)}, u32[]{:S(2)}) collective-permute-start(bf16[256,2048]{1,0:T(8,128)(2,1)S(1)} %get-tuple-element.140), channel_id=1, source_target_pairs={{64,0},{128,64},{192,128},{65,1},{129,65},{193,129},{66,2},{130,66... | collective-permute-start | bytes 3145736 | tf_op jit(solution)/shard_map/ppermute | solution.py:12
  324.0 103.8 %copy-start.3 = (bf16[256,2048]{1,0:T(8,128)(2,1)}, bf16[256,2048]{1,0:T(8,128)(2,1)S(1)}, u32[]{:S(2)}) copy-start(bf16[256,2048]{1,0:T(8,128)(2,1)S(1)} %get-tuple-element.143) | copy-start | bytes 3145732
  324.0 103.8 %collective-permute-start.5 = (bf16[256,2048]{1,0:T(8,128)(2,1)S(1)}, bf16[256,2048]{1,0:T(8,128)(2,1)S(1)}, u32[]{:S(2)}, u32[]{:S(2)}) collective-permute-start(bf16[256,2048]{1,0:T(8,128)(2,1)S(1)} %get-tuple-element.141), channel_id=1, source_target_pairs={{64,0},{128,64},{192,128},{65,1},{129,65},{193,129},{66,2},{130,66... | collective-permute-start | bytes 3145736 | tf_op jit(solution)/shard_map/ppermute | solution.py:12
Sparse Core Ops, SparseCore 0:
  9.2 117.7 all-gather.2
  440.1 325.8 reduce-scatter.1
where the time goes:
time: 777 us; the launch traced here: 773 us
  waiting for transfers between devices  681 us (88%)
  starting transfers between devices  26.6 us (3%)
  matrix products  17.7 us (2%)
  other arithmetic  17.3 us (2%)
  local copies, waits for them, and re-layouts  16.4 us (2%)
  between operations  13.5 us (2%)
    reduce_scatter x1, waiting for transfers between devices, gradient_share(): lax.psum_scatter(lax.dot_general(normed, grad_pre, (((0,), (0,)), ((), ()...  326 us
    ppermute x6, waiting for transfers between devices, shifted(): return lax.ppermute(block, axis, route)  237 us
    all_gather x1, waiting for transfers between devices, local(): gathered = lax.all_gather(weights[0], 'fsdp', axis=0, tiled=True)  117 us
    ppermute x6, starting transfers between devices, shifted(): return lax.ppermute(block, axis, route)  26.5 us
  transfers between devices with their start and end apart: 8, of which 8 were waited for; matrix products, arithmetic and copies ran while one was open for 0% of the time, Pallas kernels for 0%

commit v1 on v0

v1 whole, which is shorter than its diff:
```python
import functools

import jax
import jax.numpy as jnp
from jax import lax
from jax.experimental import pallas as pl
from jax.experimental.pallas import tpu as pltpu
from jax.sharding import PartitionSpec as P

MESH = pl.DeviceIdType.MESH
F32 = jnp.float32
BF16 = jnp.bfloat16
EPS = 1e-06
GELU_C = 0.7978845608028654
GELU_A = 0.044715

D = 2048
ROWS = 256
HALF = 1024
UNITS = 8
FIRST, SECOND = pl.ds(0, 2), pl.ds(2, 2)
TOP, BOTTOM = pl.ds(0, 32), pl.ds(32, 32)


def position():
    s, f = lax.axis_index("section"), lax.axis_index("fsdp")
    c = lax.rem(f, 2)
    x = lax.rem(f // 2, 4)
    y = lax.rem(f // 8, 4)
    zl = f // 32
    return s, zl, x, y, c


def device(x, y, z, c):
    return (z // 2, lax.rem(z, 2) * 32 + y * 8 + x * 2 + c)


def remote(src, dst, send, recv, dev):
    return pltpu.make_async_remote_copy(
        src_ref=src, dst_ref=dst, send_sem=send, recv_sem=recv, device_id=dev, device_id_type=MESH
    )


def kernel(
    x_ref, w_ref, cot_ref, len_ref, out_ref,
    wb, xs, gd, iv, gp, nw, gw, gr, gn, r1, r2, t1, t2, z1, sf, o1,
    loc, xsend, xrecv, rsend, rrecv, psend, precv, qsend, qrecv, dsend, drecv,
    nsend, nrecv, r1s, r1r, r2s, r2r, t1s, t1r, t2s, t2r, zsend, zrecv, osend, orecv,
):
    s, zl, x, y, c = position()
    z = 2 * s + zl
    sib = device(x, y, z, 1 - c)
    xp, xm = lax.rem(x + 1, 4), lax.rem(x + 3, 4)
    yp, ym = lax.rem(y + 1, 4), lax.rem(y + 3, 4)
    x2, y2 = lax.rem(x + 2, 4), lax.rem(y + 2, 4)
    dxp, dxm = device(xp, y, z, c), device(xm, y, z, c)
    dyp, dym = device(x, yp, z, c), device(x, ym, z, c)

    barrier = pltpu.get_barrier_semaphore()
    for partner in (dxp, dxm, dyp, dym, sib):
        pl.semaphore_signal(barrier, inc=1, device_id=partner, device_id_type=MESH)
    for d in range(1, 8):
        pl.semaphore_signal(
            barrier, inc=1, device_id=device(x, y, lax.rem(z + d, 8), c), device_id_type=MESH
        )

    in_x = pltpu.make_async_copy(x_ref, xs.at[0], loc.at[0])
    in_x.start()
    mine = pl.ds(pl.multiple_of(c * HALF, HALF), HALF)
    other = pl.ds(pl.multiple_of((1 - c) * HALF, HALF), HALF)
    my_rows = pl.ds(pl.multiple_of(c * 32, 32), 32)
    sib_rows = pl.ds(pl.multiple_of((1 - c) * 32, 32), 32)
    in_w = pltpu.make_async_copy(
        w_ref.at[:, mine], wb.at[2 * s + c, zl, y, x, my_rows], loc.at[1]
    )
    in_w.start()
    for m in range(2):
        for q in range(2):
            rows = pl.ds(128 * m + 64 * q, 64)
            live = lax.broadcasted_iota(jnp.int32, (64, D), 0) < len_ref[m, q]
            gr[rows, :] = jnp.where(live, cot_ref[rows, :].astype(F32), 0.0).astype(BF16)
    pl.semaphore_wait(barrier, 12)

    give = remote(
        w_ref.at[:, other], wb.at[2 * s + 1 - c, zl, y, x, my_rows], xsend, xrecv, sib
    )
    give.start()
    in_x.wait()
    in_w.wait()
    remote(
        w_ref.at[:, mine], wb.at[2 * s + c, zl, y, x, sib_rows], xsend, xrecv, sib
    ).wait_recv()

    def raw(d):
        block = wb.at[2 * s + c, zl, y, x]
        dest = device(x, y, lax.rem(z + d, 8), c)
        return remote(block, block, rsend.at[d - 1], rrecv.at[z], dest)

    def row(cc, kh, uz, i, part=None):
        if cc == 0:
            return wb.at[kh, uz, i] if part is None else wb.at[kh, uz, i, part]
        return wb.at[kh, uz, :, i] if part is None else wb.at[kh, uz, part, i]

    def chip(cc, kh, uz, i, part=None):
        at = (kh, uz, y, i) if cc == 0 else (kh, uz, i, x)
        return wb.at[at] if part is None else wb.at[at + (part,)]

    def p_copies(cc, u):
        kh, uz = 2 * (u // 2) + cc, lax.rem(u, 2)
        me, plus, minus = (x, xp, xm) if cc == 0 else (y, yp, ym)
        to_plus, to_minus = (dxp, dxm) if cc == 0 else (dyp, dym)
        own = chip(cc, kh, uz, me)
        from_minus, from_plus = chip(cc, kh, uz, minus, TOP), chip(cc, kh, uz, plus, BOTTOM)
        return (
            remote(own, own, psend.at[u, 0], precv.at[u, 0], to_plus),
            remote(own, own, psend.at[u, 1], precv.at[u, 1], to_minus),
            remote(from_minus, from_minus, psend.at[u, 2], precv.at[u, 2], to_plus),
            remote(from_plus, from_plus, psend.at[u, 3], precv.at[u, 3], to_minus),
        )

    def p_landed(cc, u, i):
        kh, uz = 2 * (u // 2) + cc, lax.rem(u, 2)
        plus, minus, far = (xp, xm, x2) if cc == 0 else (yp, ym, y2)
        land = (
            chip(cc, kh, uz, minus),
            chip(cc, kh, uz, plus),
            chip(cc, kh, uz, far, TOP),
            chip(cc, kh, uz, far, BOTTOM),
        )[i]
        remote(land, land, psend.at[u, i], precv.at[u, i], sib).wait_recv()

    def q_copies(cc, u):
        kh, uz = 2 * (u // 2) + cc, lax.rem(u, 2)
        me, plus, minus = (y, yp, ym) if cc == 0 else (x, xp, xm)
        to_plus, to_minus = (dyp, dym) if cc == 0 else (dxp, dxm)
        own = row(cc, kh, uz, me)
        from_minus, from_plus = row(cc, kh, uz, minus, FIRST), row(cc, kh, uz, plus, SECOND)
        return (
            remote(own, own, qsend.at[u, 0], qrecv.at[u, 0], to_plus),
            remote(own, own, qsend.at[u, 1], qrecv.at[u, 1], to_minus),
            remote(from_minus, from_minus, qsend.at[u, 2], qrecv.at[u, 2], to_plus),
            remote(from_plus, from_plus, qsend.at[u, 3], qrecv.at[u, 3], to_minus),
        )

    def q_landed(cc, u, i):
        kh, uz = 2 * (u // 2) + cc, lax.rem(u, 2)
        plus, minus, far = (yp, ym, y2) if cc == 0 else (xp, xm, x2)
        land = (
            row(cc, kh, uz, minus),
            row(cc, kh, uz, plus),
            row(cc, kh, uz, far, FIRST),
            row(cc, kh, uz, far, SECOND),
        )[i]
        remote(land, land, qsend.at[u, i], qrecv.at[u, i], sib).wait_recv()

    def d_copy(cc, u, i):
        kh, uz = 2 * (u // 2) + cc, lax.rem(u, 2)
        at = ((y, ym, yp, y2) if cc == 0 else (x, xm, xp, x2))[i]
        block = row(cc, kh, uz, at)
        return remote(block, block, dsend.at[u, i], drecv.at[u, i], sib)

    def unit(t):
        return jnp.where(t == 0, z, jnp.where(t - 1 < z, t - 1, t))

    def by_core(body):
        for cc in (0, 1):
            pl.when(c == cc)(functools.partial(body, cc))

    def stage_p1(t):
        u = unit(t)

        @pl.when(t == 0)
        def _():
            for d in (1, 7, 2, 6, 3, 5, 4):
                raw(d).start()

        @pl.when(t > 0)
        def _():
            block = wb.at[2 * (u // 2) + c, lax.rem(u, 2), y, x]
            remote(block, block, rsend.at[0], rrecv.at[u], sib).wait_recv()

        def body(cc):
            copies = p_copies(cc, u)
            copies[0].start()
            copies[1].start()

        by_core(body)

    def stage_p2(t):
        u = unit(t)

        def body(cc):
            copies = p_copies(cc, u)
            p_landed(cc, u, 0)
            copies[2].start()
            p_landed(cc, u, 1)
            copies[3].start()

        by_core(body)

    def stage_q1(t):
        u = unit(t)

        def body(cc):
            copies = q_copies(cc, u)
            p_landed(cc, u, 2)
            p_landed(cc, u, 3)
            copies[0].start()
            copies[1].start()
            d_copy(cc, u, 0).start()

        by_core(body)

    def stage_q2(t):
        u = unit(t)

        def body(cc):
            copies = q_copies(cc, u)
            q_landed(cc, u, 0)
            copies[2].start()
            q_landed(cc, u, 1)
            copies[3].start()
            d_copy(cc, u, 1).start()
            d_copy(cc, u, 2).start()

        by_core(body)

    def stage_f(t):
        u = unit(t)

        def body(cc):
            q_landed(cc, u, 2)
            q_landed(cc, u, 3)
            d_copy(cc, u, 3).start()

        by_core(body)

    def normed_copy():
        return remote(nw.at[c], nw.at[c], nsend.at[0], nrecv.at[0], sib)

    def forward(k):
        def body(cc):
            @pl.loop(0, 2)
            def _(uz):
                for i in range(4):
                    d_copy(1 - cc, 2 * k + uz, i).wait_recv()

        by_core(body)

        @pl.loop(0, ROWS // 32)
        def _(i):
            rows = pl.ds(pl.multiple_of(i * 32, 32), 32)
            xf = xs[k, rows, :].astype(F32)
            inv = lax.rsqrt(jnp.mean(xf * xf, axis=-1, keepdims=True) + EPS)
            iv[k, rows, :] = jnp.broadcast_to(inv, (32, 128))
            gp[rows, :] = (xf * inv).astype(BF16)

        @pl.when(k == s)
        def _():
            nw[c] = gp[...]
            normed_copy().start()

        @pl.loop(0, 4)
        def _(j):
            inside = pl.ds(pl.multiple_of(lax.rem(j, 2) * 512, 512), 512)
            cols = pl.ds(pl.multiple_of(j * 512, 512), 512)
            w = wb[2 * k + j // 2, :, :, :, :, inside].reshape(D, 512)
            u = jnp.dot(gp[...], w, preferred_element_type=F32)
            uu = u * u
            t = jnp.tanh((GELU_C * u) * (1.0 + GELU_A * uu))
            cdf = 0.5 * (1.0 + t)
            gd[k, :, cols] = cdf + (0.5 * GELU_C) * u * (1.0 - t * t) * (
                1.0 + (3.0 * GELU_A) * uu
            )

            @pl.when(k < 3)
            def _():
                nxt = jnp.minimum(k + 1, 3)
                xs[nxt, :, cols] = (xs[k, :, cols].astype(F32) + u * cdf).astype(BF16)

    @pl.loop(0, UNITS + 4)
    def _(i):
        pl.when(i < UNITS)(lambda: stage_p1(i))
        pl.when((i >= 1) & (i < UNITS + 1))(lambda: stage_p2(i - 1))
        pl.when((i >= 2) & (i < UNITS + 2))(lambda: stage_q1(i - 2))
        pl.when((i >= 3) & (i < UNITS + 3))(lambda: stage_q2(i - 3))
        pl.when(i >= 4)(lambda: stage_f(i - 4))
        ready = (i == 6) | (i == 8) | (i == 10) | (i == 11)
        k = jnp.where(i == 11, 3, (jnp.maximum(i, 6) - 6) // 2)
        pl.when(ready)(lambda: forward(k))

    def grad_pre(k):
        @pl.loop(0, ROWS // 32)
        def _(i):
            rows = pl.ds(pl.multiple_of(i * 32, 32), 32)
            gp[rows, :] = (gr[rows, :].astype(F32) * gd[k, rows, :]).astype(BF16)

    @pl.loop(0, 3 - s)
    def _(step):
        k = 3 - step
        grad_pre(k)

        @pl.loop(0, 4)
        def _(j):
            total = None
            for h in range(2):
                w = wb[2 * k + h, j // 2, pl.ds(lax.rem(j, 2) * 2, 2)].reshape(512, HALF)
                part = lax.dot_general(
                    gp[:, h * HALF : (h + 1) * HALF], w, (((1,), (1,)), ((), ())),
                    preferred_element_type=F32,
                )
                total = part if total is None else total + part
            gn[:, pl.ds(pl.multiple_of(j * 512, 512), 512)] = total

        @pl.loop(0, ROWS // 32)
        def _(i):
            rows = pl.ds(pl.multiple_of(i * 32, 32), 32)
            xf = xs[k, rows, :].astype(F32)
            g = gn[rows, :]
            inv = iv[k, rows, :][:, :1]
            mean = jnp.mean(g * xf, axis=-1, keepdims=True)
            gr[rows, :] = (
                gr[rows, :].astype(F32) + inv * g - xf * (inv * inv * inv * mean)
            ).astype(BF16)

    grad_pre(s)
    gw[c] = gp[:, mine]
    give_g = remote(gp.at[:, other], gw.at[c], nsend.at[1], nrecv.at[1], sib)
    give_g.start()

    give.wait_send()
    for d in range(1, 8):
        raw(d).wait_send()

    @pl.loop(0, UNITS)
    def _(u):
        def body(cc):
            for copy in p_copies(cc, u) + q_copies(cc, u):
                copy.wait_send()
            for i in range(4):
                d_copy(cc, u, i).wait_send()

        by_core(body)

    remote(nw.at[1 - c], nw.at[1 - c], nsend.at[0], nrecv.at[0], sib).wait_recv()
    remote(gw.at[1 - c], gw.at[1 - c], nsend.at[1], nrecv.at[1], sib).wait_recv()

    gb = wb.at[0]

    def weight_term(v):
        @pl.loop(0, 4)
        def _(j):
            cols = pl.ds(pl.multiple_of(v * HALF + j * 256, 256), 256)
            total = None
            for half in range(2):
                part = lax.dot_general(
                    nw[half, :, cols], gw[half], (((0,), (0,)), ((), ())),
                    preferred_element_type=F32,
                )
                total = part if total is None else total + part
            gb[v, j] = total.astype(BF16).reshape(4, 64, HALF)

    def grow(cc, v, i, part=None):
        if cc == 0:
            return gb.at[v, i] if part is None else gb.at[v, i, part]
        return gb.at[v, :, i] if part is None else gb.at[v, part, i]

    def gchip(cc, v, i, part=None):
        at = (v, y, i) if cc == 0 else (v, i, x)
        return gb.at[at] if part is None else gb.at[at + (part,)]

    def r1_copies(cc, v):
        far = y2 if cc == 0 else x2
        to_plus, to_minus = (dyp, dym) if cc == 0 else (dxp, dxm)
        return (
            remote(grow(cc, v, far, FIRST), r1.at[v, 0], r1s.at[v, 0], r1r.at[v, 0], to_plus),
            remote(grow(cc, v, far, SECOND), r1.at[v, 1], r1s.at[v, 1], r1r.at[v, 1], to_minus),
        )

    def r2_copies(cc, v):
        plus, minus = (yp, ym) if cc == 0 else (xp, xm)
        to_plus, to_minus = (dyp, dym) if cc == 0 else (dxp, dxm)
        return (
            remote(grow(cc, v, plus), r2.at[v, 0], r2s.at[v, 0], r2r.at[v, 0], to_plus),
            remote(grow(cc, v, minus), r2.at[v, 1], r2s.at[v, 1], r2r.at[v, 1], to_minus),
        )

    def t1_copies(cc, v):
        far = x2 if cc == 0 else y2
        to_plus, to_minus = (dxp, dxm) if cc == 0 else (dyp, dym)
        return (
            remote(gchip(cc, v, far, TOP), t1.at[v, 0], t1s.at[v, 0], t1r.at[v, 0], to_plus),
            remote(gchip(cc, v, far, BOTTOM), t1.at[v, 1], t1s.at[v, 1], t1r.at[v, 1], to_minus),
        )

    def t2_copies(cc, v):
        plus, minus = (xp, xm) if cc == 0 else (yp, ym)
        to_plus, to_minus = (dxp, dxm) if cc == 0 else (dyp, dym)
        return (
            remote(gchip(cc, v, plus), t2.at[v, 0], t2s.at[v, 0], t2r.at[v, 0], to_plus),
            remote(gchip(cc, v, minus), t2.at[v, 1], t2s.at[v, 1], t2r.at[v, 1], to_minus),
        )

    def add_into(ref, *others):
        total = ref[...].astype(F32)
        for more in others:
            total = total + more[...].astype(F32)
        ref[...] = total.astype(BF16)

    def rs_a(v):
        def body(cc):
            for copy in r1_copies(cc, v):
                copy.start()

        by_core(body)

    def rs_b(v):
        def body(cc):
            plus, minus = (yp, ym) if cc == 0 else (xp, xm)
            arrive, leave = r1_copies(cc, v), r2_copies(cc, v)
            arrive[0].wait_recv()
            add_into(grow(cc, v, plus, FIRST), r1.at[v, 0])
            leave[0].start()
            arrive[1].wait_recv()
            add_into(grow(cc, v, minus, SECOND), r1.at[v, 1])
            leave[1].start()

        by_core(body)

    def rs_c(v):
        def body(cc):
            me = y if cc == 0 else x
            arrive, leave = r2_copies(cc, v), t1_copies(cc, v)
            arrive[0].wait_recv()
            arrive[1].wait_recv()
            for i in range(4):
                block = gchip(cc, v, i)
                add_into(block, r2.at[v, 0, i], r2.at[v, 1, i])
            for copy in leave:
                copy.start()

        by_core(body)

    def rs_d(v):
        def body(cc):
            plus, minus = (xp, xm) if cc == 0 else (yp, ym)
            arrive, leave = t1_copies(cc, v), t2_copies(cc, v)
            arrive[0].wait_recv()
            add_into(gchip(cc, v, plus, TOP), t1.at[v, 0])
            leave[0].start()
            arrive[1].wait_recv()
            add_into(gchip(cc, v, minus, BOTTOM), t1.at[v, 1])
            leave[1].start()

        by_core(body)

    def rs_e(v):
        def body(cc):
            for copy in t2_copies(cc, v):
                copy.wait_recv()

        by_core(body)
        return (
            gb[v, y, x].astype(F32) + t2[v, 0].astype(F32) + t2[v, 1].astype(F32)
        )

    v0, v1 = 1 - zl, zl
    weight_term(v0)
    rs_a(v0)
    weight_term(v1)
    rs_a(v1)
    rs_b(v0)
    rs_b(v1)
    rs_c(v0)
    rs_c(v1)
    rs_d(v0)
    rs_d(v1)
    gb[v0, y, x] = rs_e(v0).astype(BF16)
    pair = device(x, y, 2 * s + 1 - zl, c)
    cross = remote(gb.at[v0, y, x], z1, zsend, zrecv, pair)
    cross.start()
    sf[...] = rs_e(v1)
    cross.wait_recv()
    sf[...] = sf[...] + z1[...].astype(F32)
    last = remote(sf.at[sib_rows], o1, osend, orecv, sib)
    last.start()
    out_ref[:, mine] = sf[my_rows, :]
    last.wait_recv()
    out_ref[:, other] = o1[...]

    last.wait_send()
    cross.wait_send()
    give_g.wait_send()
    normed_copy().wait_send()

    @pl.loop(0, 2)
    def _(v):
        def body(cc):
            for copies in (r1_copies, r2_copies, t1_copies, t2_copies):
                for copy in copies(cc, v):
                    copy.wait_send()

        by_core(body)


def local(inputs, weights, cotangents, lengths):
    rows = inputs.shape[0] * inputs.shape[1]
    dma = pltpu.SemaphoreType.DMA
    vmem = pl.BlockSpec(memory_space=pltpu.VMEM)
    out = pl.pallas_call(
        kernel,
        out_shape=jax.ShapeDtypeStruct((32, D), F32),
        in_specs=[
            pl.BlockSpec(memory_space=pl.ANY),
            vmem,
            vmem,
            pl.BlockSpec(memory_space=pltpu.SMEM),
        ],
        out_specs=vmem,
        scratch_shapes=[
            pltpu.VMEM((8, 2, 4, 4, 64, HALF), BF16),
            pltpu.VMEM((4, ROWS, D), BF16),
            pltpu.VMEM((4, ROWS, D), F32),
            pltpu.VMEM((4, ROWS, 128), F32),
            pltpu.VMEM((ROWS, D), BF16),
            pltpu.VMEM((2, ROWS, D), BF16),
            pltpu.VMEM((2, ROWS, HALF), BF16),
            pltpu.VMEM((ROWS, D), BF16),
            pltpu.VMEM((ROWS, D), F32),
            pltpu.VMEM((2, 2, 2, 64, HALF), BF16),
            pltpu.VMEM((2, 2, 4, 64, HALF), BF16),
            pltpu.VMEM((2, 2, 32, HALF), BF16),
            pltpu.VMEM((2, 2, 64, HALF), BF16),
            pltpu.VMEM((64, HALF), BF16),
            pltpu.VMEM((64, HALF), F32),
            pltpu.VMEM((32, HALF), F32),
            dma((2,)),
            dma,
            dma,
            dma((7,)),
            dma((8,)),
            dma((8, 4)),
            dma((8, 4)),
            dma((8, 4)),
            dma((8, 4)),
            dma((8, 4)),
            dma((8, 4)),
            dma((2,)),
            dma((2,)),
            dma((2, 2)),
            dma((2, 2)),
            dma((2, 2)),
            dma((2, 2)),
            dma((2, 2)),
            dma((2, 2)),
            dma((2, 2)),
            dma((2, 2)),
            dma,
            dma,
            dma,
            dma,
        ],
        compiler_params=pltpu.CompilerParams(
            collective_id=0, has_side_effects=True, vmem_limit_bytes=62 * 2**20
        ),
        cost_estimate=pl.CostEstimate(
            flops=9 * 2 * ROWS * D * D, bytes_accessed=36 * 2**20, transcendentals=4 * ROWS * D
        ),
    )(inputs.reshape(rows, D), weights[0], cotangents.reshape(rows, D), lengths)
    return out[None]


def solution(mesh):
    in_specs = (
        P(None, "fsdp", None),
        P("section", "fsdp", None),
        P(None, "fsdp", None),
        P(None, "fsdp"),
    )
    out_specs = P("section", "fsdp", None)
    return jax.shard_map(local, mesh=mesh, in_specs=in_specs, out_specs=out_specs, check_vma=False)
```

time: 777 us -> 174 us (0.22)
  the two profiles are of different devices: /device:TPU:1 before, /device:TPU:161 now
where the time goes in v1:
time: 174 us
  Pallas kernels  172 us (99%)
    pallas_call x1, Pallas kernels, local(): pl.pallas_call(kernel, out_shape=jax.ShapeDtypeStruct((32, D), F32), in_s...  172 us

profile of v1, /device:TPU:161, one launch (start us, length us, event | category | flops | bytes accessed | tf_op | source)
XLA Modules:
  0.0 173.6 jit_solution(5388305093293349992)
XLA Ops:
  0.0 171.9 %shard_map.46 = f32[32,2048]{1,0:T(8,128)} custom-call(bf16[256,2048]{1,0:T(8,128)(2,1)} %bitcast.5, bf16[32,2048]{1,0:T(8,128)(2,1)} %bitcast.7, bf16[256,2048]{1,0:T(8,128)(2,1)} %bitcast.6, s32[2,2]{1,0:T(2,128)} %len_ref.1), custom_call_target="tpu_custom_call" | custom-call | flops 19327352832 | bytes 37748736 | tf_op jit(solution)/shard_map/pallas_call | solution.py:510
  171.9 1.7 copy.6

commit v2 on v1

v2 whole, which is shorter than its diff:
```python
import functools

import jax
import jax.numpy as jnp
from jax import lax
from jax.experimental import pallas as pl
from jax.experimental.pallas import tpu as pltpu
from jax.sharding import PartitionSpec as P

MESH = pl.DeviceIdType.MESH
F32 = jnp.float32
BF16 = jnp.bfloat16
EPS = 1e-06
GELU_C = 0.7978845608028654
GELU_A = 0.044715

D = 2048
ROWS = 256
HALF = 1024
XY = 768
Z = HALF - XY
UNITS = 8
READY = ((4, 6, 8, 9), (6, 7, 8, 9), (6, 7, 8, 9), (6, 8, 9, 10))
FIRST, SECOND = pl.ds(0, 2), pl.ds(2, 2)
TOP, BOTTOM = pl.ds(0, 32), pl.ds(32, 32)


def position():
    s, f = lax.axis_index("section"), lax.axis_index("fsdp")
    c = lax.rem(f, 2)
    x = lax.rem(f // 2, 4)
    y = lax.rem(f // 8, 4)
    zl = f // 32
    return s, zl, x, y, c


def device(x, y, z, c):
    return (z // 2, lax.rem(z, 2) * 32 + y * 8 + x * 2 + c)


def remote(src, dst, send, recv, dev):
    return pltpu.make_async_remote_copy(
        src_ref=src, dst_ref=dst, send_sem=send, recv_sem=recv, device_id=dev, device_id_type=MESH
    )


def kernel(
    x_ref, w_ref, cot_ref, len_ref, out_ref,
    wa, wz, xs, gd, iv, gp, nw, gw, gr, gn, r1, r2, t1, t2, z1, sf, o1,
    loc, xsend, xrecv, rsend, rrecv, usend, urecv, lsend, lrecv, esend, erecv, psend, precv, qsend, qrecv, dsend, drecv,
    nsend, nrecv, r1s, r1r, r2s, r2r, t1s, t1r, t2s, t2r, zsend, zrecv, osend, orecv,
):
    s, zl, x, y, c = position()
    z = 2 * s + zl
    sib = device(x, y, z, 1 - c)
    xp, xm = lax.rem(x + 1, 4), lax.rem(x + 3, 4)
    yp, ym = lax.rem(y + 1, 4), lax.rem(y + 3, 4)
    x2, y2 = lax.rem(x + 2, 4), lax.rem(y + 2, 4)
    dxp, dxm = device(xp, y, z, c), device(xm, y, z, c)
    dyp, dym = device(x, yp, z, c), device(x, ym, z, c)

    barrier = pltpu.get_barrier_semaphore()
    for partner in (dxp, dxm, dyp, dym, sib):
        pl.semaphore_signal(barrier, inc=1, device_id=partner, device_id_type=MESH)
    for d in range(1, 8):
        pl.semaphore_signal(
            barrier, inc=1, device_id=device(x, y, lax.rem(z + d, 8), c), device_id_type=MESH
        )

    def part(core, first, width):
        return pl.ds(pl.multiple_of(core * HALF + first, 256), width)

    in_x = [
        pltpu.make_async_copy(x_ref.at[:, :, h * HALF : (h + 1) * HALF], xs.at[h], loc.at[3 * h])
        for h in range(2)
    ]
    for copy in in_x:
        copy.start()
    mine = pl.ds(pl.multiple_of(c * HALF, HALF), HALF)
    other = pl.ds(pl.multiple_of((1 - c) * HALF, HALF), HALF)
    my_rows = pl.ds(pl.multiple_of(c * 32, 32), 32)
    sib_rows = pl.ds(pl.multiple_of((1 - c) * 32, 32), 32)
    in_w = [
        pltpu.make_async_copy(src, dst, loc.at[1 + i])
        for i, (src, dst) in enumerate(
            (
                (w_ref.at[:, part(c, 0, XY)], wa.at[2 * s + c, zl, y, x, my_rows]),
                (w_ref.at[:, part(c, XY, Z)], wz.at[2 * s + c, zl, y, x, my_rows]),
            )
        )
    ]
    for copy in in_w:
        copy.start()
    for m in range(2):
        for q in range(2):
            rows = pl.ds(128 * m + 64 * q, 64)
            live = lax.broadcasted_iota(jnp.int32, (64, D), 0) < len_ref[m, q]
            gr[rows, :] = jnp.where(live, cot_ref[rows, :].astype(F32), 0.0).astype(BF16)
    pl.semaphore_wait(barrier, 12)

    def gives(core, rows):
        kh = 2 * s + core
        return (
            remote(
                w_ref.at[:, part(core, XY, Z)], wz.at[kh, zl, y, x, rows],
                xsend.at[0], xrecv.at[0], sib,
            ),
            remote(
                w_ref.at[:, part(core, 0, XY)], wa.at[kh, zl, y, x, rows],
                xsend.at[1], xrecv.at[1], sib,
            ),
        )

    for copy in gives(1 - c, my_rows):
        copy.start()
    for copy in in_x + in_w:
        copy.wait()
    for copy in gives(c, sib_rows):
        copy.wait_recv()

    def raw(d):
        block = wa.at[2 * s + c, zl, y, x]
        dest = device(x, y, lax.rem(z + d, 8), c)
        return remote(block, block, rsend.at[d - 1], rrecv.at[z], dest)

    def row(w, cc, kh, uz, i, part=None):
        if cc == 0:
            return w.at[kh, uz, i] if part is None else w.at[kh, uz, i, part]
        return w.at[kh, uz, :, i] if part is None else w.at[kh, uz, part, i]

    def chip(w, cc, kh, uz, i, part=None):
        at = (kh, uz, y, i) if cc == 0 else (kh, uz, i, x)
        return w.at[at] if part is None else w.at[at + (part,)]

    def p_copies(w, cc, u, b):
        kh, uz = 2 * (u // 2) + cc, lax.rem(u, 2)
        me, plus, minus = (x, xp, xm) if cc == 0 else (y, yp, ym)
        to_plus, to_minus = (dxp, dxm) if cc == 0 else (dyp, dym)
        own = chip(w, cc, kh, uz, me)
        from_minus, from_plus = chip(w, cc, kh, uz, minus, TOP), chip(w, cc, kh, uz, plus, BOTTOM)
        return (
            remote(own, own, psend.at[b, 0], precv.at[b, 0], to_plus),
            remote(own, own, psend.at[b, 1], precv.at[b, 1], to_minus),
            remote(from_minus, from_minus, psend.at[b, 2], precv.at[b, 2], to_plus),
            remote(from_plus, from_plus, psend.at[b, 3], precv.at[b, 3], to_minus),
        )

    def p_landed(w, cc, u, b, i):
        kh, uz = 2 * (u // 2) + cc, lax.rem(u, 2)
        plus, minus, far = (xp, xm, x2) if cc == 0 else (yp, ym, y2)
        land = (
            chip(w, cc, kh, uz, minus),
            chip(w, cc, kh, uz, plus),
            chip(w, cc, kh, uz, far, TOP),
            chip(w, cc, kh, uz, far, BOTTOM),
        )[i]
        remote(land, land, psend.at[b, i], precv.at[b, i], sib).wait_recv()

    def q_copies(w, cc, u, b):
        kh, uz = 2 * (u // 2) + cc, lax.rem(u, 2)
        me, plus, minus = (y, yp, ym) if cc == 0 else (x, xp, xm)
        to_plus, to_minus = (dyp, dym) if cc == 0 else (dxp, dxm)
        own = row(w, cc, kh, uz, me)
        from_minus, from_plus = row(w, cc, kh, uz, minus, FIRST), row(w, cc, kh, uz, plus, SECOND)
        return (
            remote(own, own, qsend.at[b, 0], qrecv.at[b, 0], to_plus),
            remote(own, own, qsend.at[b, 1], qrecv.at[b, 1], to_minus),
            remote(from_minus, from_minus, qsend.at[b, 2], qrecv.at[b, 2], to_plus),
            remote(from_plus, from_plus, qsend.at[b, 3], qrecv.at[b, 3], to_minus),
        )

    def q_landed(w, cc, u, b, i):
        kh, uz = 2 * (u // 2) + cc, lax.rem(u, 2)
        plus, minus, far = (yp, ym, y2) if cc == 0 else (xp, xm, x2)
        land = (
            row(w, cc, kh, uz, minus),
            row(w, cc, kh, uz, plus),
            row(w, cc, kh, uz, far, FIRST),
            row(w, cc, kh, uz, far, SECOND),
        )[i]
        remote(land, land, qsend.at[b, i], qrecv.at[b, i], sib).wait_recv()

    def d_copy(w, cc, u, b, i):
        kh, uz = 2 * (u // 2) + cc, lax.rem(u, 2)
        at = ((y, ym, yp, y2) if cc == 0 else (x, xm, xp, x2))[i]
        block = row(w, cc, kh, uz, at)
        return remote(block, block, dsend.at[b, i], drecv.at[b, i], sib)

    def by_core(body):
        for cc in (0, 1):
            pl.when(c == cc)(functools.partial(body, cc))

    def unit(t):
        rest = t - 2
        rest = jnp.where(rest < 2 * s, rest, rest + 2)
        return jnp.where(t == 0, z, jnp.where(t == 1, 2 * s + 1 - zl, rest))

    def stage_p1(w, u, b):
        def body(cc):
            copies = p_copies(w, cc, u, b)
            copies[0].start()
            copies[1].start()

        by_core(body)

    def raw_landed(u):
        block = wa.at[2 * (u // 2) + c, lax.rem(u, 2), y, x]
        remote(block, block, rsend.at[0], rrecv.at[u], sib).wait_recv()

    def stage_p2(w, u, b):
        def body(cc):
            copies = p_copies(w, cc, u, b)
            p_landed(w, cc, u, b, 0)
            copies[2].start()
            p_landed(w, cc, u, b, 1)
            copies[3].start()

        by_core(body)

    def stage_q1(w, u, b):
        def body(cc):
            copies = q_copies(w, cc, u, b)
            p_landed(w, cc, u, b, 2)
            p_landed(w, cc, u, b, 3)
            copies[0].start()
            copies[1].start()
            d_copy(w, cc, u, b, 0).start()

        by_core(body)

    def stage_q2(w, u, b):
        def body(cc):
            copies = q_copies(w, cc, u, b)
            q_landed(w, cc, u, b, 0)
            copies[2].start()
            q_landed(w, cc, u, b, 1)
            copies[3].start()
            d_copy(w, cc, u, b, 1).start()
            d_copy(w, cc, u, b, 2).start()

        by_core(body)

    def stage_f(w, u, b):
        def body(cc):
            q_landed(w, cc, u, b, 2)
            q_landed(w, cc, u, b, 3)
            d_copy(w, cc, u, b, 3).start()

        by_core(body)

    PARTS = (pl.ds(0, 2), pl.ds(2, 2))
    above, below = device(x, y, lax.rem(z + 1, 8), c), device(x, y, lax.rem(z + 7, 8), c)

    def plane(d, part, core=None):
        v = lax.rem(z + 8 + d, 8)
        core = c if core is None else core
        return wz.at[2 * (v // 2) + core, lax.rem(v, 2), PARTS[part]]

    def up(r, part):
        block = plane(1 - r, part)
        return remote(block, block, usend.at[r - 1, part], urecv.at[r - 1, part], above)

    def down(r, part):
        block = plane(r - 1, part)
        return remote(block, block, lsend.at[r - 1, part], lrecv.at[r - 1, part], below)

    def up_landed(r, part):
        block = plane(-r, part)
        remote(block, block, usend.at[r - 1, part], urecv.at[r - 1, part], above).wait_recv()

    def down_landed(r, part):
        block = plane(r, part)
        remote(block, block, lsend.at[r - 1, part], lrecv.at[r - 1, part], below).wait_recv()

    def e_copy(slot, part):
        d = (-1, -2, -3, 1, 2, 3, 4)[slot]
        block = plane(d, part)
        return remote(block, block, esend.at[slot, part], erecv.at[slot, part], sib)

    def relay(r, part):
        up_landed(r, part)
        if r < 3 or part == 0:
            up(r + 1, part).start()
        down_landed(r, part)
        if r < 3 or part == 1:
            down(r + 1, part).start()
        e_copy(r - 1, part).start()
        e_copy(r + 2, part).start()

    def relay_end():
        up_landed(4, 0)
        e_copy(6, 0).start()
        down_landed(4, 1)
        e_copy(6, 1).start()

    def normed_copy():
        return remote(nw.at[c], nw.at[c], nsend.at[0], nrecv.at[0], sib)

    def section_rows(k, i):
        at = pl.ds(pl.multiple_of(lax.rem(i, 2) * 32, 32), 32)
        halves = [xs[2 * k + h, i // 2, at, :].astype(F32) for h in range(2)]
        return jnp.concatenate(halves, axis=1)

    def forward(k):
        @pl.loop(0, 2)
        def _(uz):
            u = 2 * k + uz

            def body(cc):
                for i in range(4):
                    d_copy(wa, 1 - cc, u, u, i).wait_recv()

                @pl.when(u == z)
                def _():
                    for i in range(4):
                        d_copy(wz, 1 - cc, u, UNITS, i).wait_recv()

            by_core(body)

            @pl.when(u != z)
            def _():
                d = lax.rem(u - z + 8, 8)
                slot = jnp.where(d < 4, 2 + d, jnp.where(d == 4, 6, 7 - d))
                for i in range(2):
                    block = wz.at[2 * k + 1 - c, uz, PARTS[i]]
                    remote(block, block, esend.at[slot, i], erecv.at[slot, i], sib).wait_recv()

        @pl.loop(0, ROWS // 32)
        def _(i):
            rows = pl.ds(pl.multiple_of(i * 32, 32), 32)
            xf = section_rows(k, i)
            inv = lax.rsqrt(jnp.mean(xf * xf, axis=-1, keepdims=True) + EPS)
            iv[k, rows, :] = jnp.broadcast_to(inv, (32, 128))
            gp[rows, :] = (xf * inv).astype(BF16)

        @pl.when(k == s)
        def _():
            nw[c] = gp[...]
            normed_copy().start()

        def section_columns(w, h, first, width):
            cols = part(h, first, width)
            u = jnp.dot(gp[...], w.reshape(D, width), preferred_element_type=F32)
            uu = u * u
            t = jnp.tanh((GELU_C * u) * (1.0 + GELU_A * uu))
            cdf = 0.5 * (1.0 + t)
            gd[k, :, cols] = cdf + (0.5 * GELU_C) * u * (1.0 - t * t) * (
                1.0 + (3.0 * GELU_A) * uu
            )

            @pl.when(k < 3)
            def _():
                nxt = jnp.minimum(k + 1, 3)
                inside = pl.ds(first, width)
                before = xs[2 * k + h, :, :, inside].reshape(ROWS, width)
                after = (before.astype(F32) + u * cdf).astype(BF16)
                xs[2 * nxt + h, :, :, inside] = after.reshape(4, 64, width)

        @pl.loop(0, 2)
        def _(h):
            section_columns(wa[2 * k + h], h, 0, XY)
            section_columns(wz[2 * k + h], h, XY, Z)

    own = unit(0)
    stage_p1(wz, own, UNITS)
    stage_p1(wa, own, own)
    for d in (1, 7, 2, 6, 3, 5, 4):
        raw(d).start()
    stage_p2(wz, own, UNITS)
    stage_p2(wa, own, own)
    stage_q1(wz, own, UNITS)
    stage_q1(wa, own, own)
    near = unit(1)
    raw_landed(near)
    stage_p1(wa, near, near)
    stage_q2(wz, own, UNITS)
    stage_f(wz, own, UNITS)
    for part_ in range(2):
        up(1, part_).start()
        down(1, part_).start()
    stage_p2(wa, near, near)

    @pl.loop(1, UNITS + 3)
    def _(i):
        def when_unit(ahead, stage):
            @pl.when((i + ahead >= 0) & (i + ahead < UNITS))
            def _():
                u = unit(i + ahead)
                stage(wa, u, u)

        def first_stage(w, u, b):
            raw_landed(u)
            stage_p1(w, u, b)

        when_unit(1, first_stage)
        when_unit(0, stage_q1)
        when_unit(1, stage_p2)
        when_unit(-1, stage_q2)
        when_unit(-2, stage_f)
        pl.when(i == 1)(lambda: relay(1, 0))
        pl.when(i == 2)(lambda: relay(1, 1))
        pl.when(i == 3)(lambda: relay(2, 0))
        pl.when(i == 4)(lambda: relay(2, 1))

        @pl.when(i == 5)
        def _():
            relay(3, 0)
            relay(3, 1)

        pl.when(i == 6)(relay_end)
        k = -1
        for section in range(4):
            for number in range(4):
                k = jnp.where((s == section) & (i == READY[section][number]), number, k)
        pl.when(k >= 0)(lambda: forward(jnp.maximum(k, 0)))

    def grad_pre(k):
        @pl.loop(0, ROWS // 32)
        def _(i):
            rows = pl.ds(pl.multiple_of(i * 32, 32), 32)
            gp[rows, :] = (gr[rows, :].astype(F32) * gd[k, rows, :]).astype(BF16)

    @pl.loop(0, 3 - s)
    def _(step):
        k = 3 - step
        grad_pre(k)

        @pl.loop(0, 4)
        def _(j):
            total = None
            for h in range(2):
                for w, first, width in ((wa, 0, XY), (wz, XY, Z)):
                    tile = w[2 * k + h, j // 2, pl.ds(lax.rem(j, 2) * 2, 2)].reshape(512, width)
                    term = lax.dot_general(
                        gp[:, h * HALF + first : h * HALF + first + width], tile,
                        (((1,), (1,)), ((), ())), preferred_element_type=F32,
                    )
                    total = term if total is None else total + term
            gn[:, pl.ds(pl.multiple_of(j * 512, 512), 512)] = total

        @pl.loop(0, ROWS // 32)
        def _(i):
            rows = pl.ds(pl.multiple_of(i * 32, 32), 32)
            xf = section_rows(k, i)
            g = gn[rows, :]
            inv = iv[k, rows, :][:, :1]
            mean = jnp.mean(g * xf, axis=-1, keepdims=True)
            gr[rows, :] = (
                gr[rows, :].astype(F32) + inv * g - xf * (inv * inv * inv * mean)
            ).astype(BF16)

    grad_pre(s)
    gw[c] = gp[:, mine]
    give_g = remote(gp.at[:, other], gw.at[c], nsend.at[1], nrecv.at[1], sib)
    give_g.start()

    remote(nw.at[1 - c], nw.at[1 - c], nsend.at[0], nrecv.at[0], sib).wait_recv()
    remote(gw.at[1 - c], gw.at[1 - c], nsend.at[1], nrecv.at[1], sib).wait_recv()

    def weight_term(v):
        @pl.loop(0, 4)
        def _(j):
            cols = pl.ds(pl.multiple_of(v * HALF + j * 256, 256), 256)
            total = None
            for half in range(2):
                part = lax.dot_general(
                    nw[half, :, cols], gw[half], (((0,), (0,)), ((), ())),
                    preferred_element_type=F32,
                )
                total = part if total is None else total + part
            xs[4 * v + j] = total.astype(BF16).reshape(4, 64, HALF)

    def grow(cc, v, i, first=0, count=4):
        if cc == 0:
            return xs.at[4 * v + i, pl.ds(first, count)]
        return xs.at[pl.ds(4 * v + first, count), i]

    def gchip(cc, v, i, part=None):
        at = (4 * v + y, i) if cc == 0 else (4 * v + i, x)
        return xs.at[at] if part is None else xs.at[at + (part,)]

    def r1_copies(cc, v):
        far = y2 if cc == 0 else x2
        to_plus, to_minus = (dyp, dym) if cc == 0 else (dxp, dxm)
        return (
            remote(grow(cc, v, far, 0, 2), r1.at[v, 0], r1s.at[v, 0], r1r.at[v, 0], to_plus),
            remote(grow(cc, v, far, 2, 2), r1.at[v, 1], r1s.at[v, 1], r1r.at[v, 1], to_minus),
        )

    def r2_copies(cc, v):
        plus, minus = (yp, ym) if cc == 0 else (xp, xm)
        to_plus, to_minus = (dyp, dym) if cc == 0 else (dxp, dxm)
        return (
            remote(grow(cc, v, plus), r2.at[v, 0], r2s.at[v, 0], r2r.at[v, 0], to_plus),
            remote(grow(cc, v, minus), r2.at[v, 1], r2s.at[v, 1], r2r.at[v, 1], to_minus),
        )

    def t1_copies(cc, v):
        far = x2 if cc == 0 else y2
        to_plus, to_minus = (dxp, dxm) if cc == 0 else (dyp, dym)
        return (
            remote(gchip(cc, v, far, TOP), t1.at[v, 0], t1s.at[v, 0], t1r.at[v, 0], to_plus),
            remote(gchip(cc, v, far, BOTTOM), t1.at[v, 1], t1s.at[v, 1], t1r.at[v, 1], to_minus),
        )

    def t2_copies(cc, v):
        plus, minus = (xp, xm) if cc == 0 else (yp, ym)
        to_plus, to_minus = (dxp, dxm) if cc == 0 else (dyp, dym)
        return (
            remote(gchip(cc, v, plus), t2.at[v, 0], t2s.at[v, 0], t2r.at[v, 0], to_plus),
            remote(gchip(cc, v, minus), t2.at[v, 1], t2s.at[v, 1], t2r.at[v, 1], to_minus),
        )

    def add_into(ref, *others):
        total = ref[...].astype(F32)
        for more in others:
            total = total + more[...].astype(F32)
        ref[...] = total.astype(BF16)

    def rs_a(v):
        def body(cc):
            for copy in r1_copies(cc, v):
                copy.start()

        by_core(body)

    def rs_b(v):
        def body(cc):
            plus, minus = (yp, ym) if cc == 0 else (xp, xm)
            arrive, leave = r1_copies(cc, v), r2_copies(cc, v)
            arrive[0].wait_recv()
            add_into(grow(cc, v, plus, 0, 2), r1.at[v, 0])
            leave[0].start()
            arrive[1].wait_recv()
            add_into(grow(cc, v, minus, 2, 2), r1.at[v, 1])
            leave[1].start()

        by_core(body)

    def rs_c(v):
        def body(cc):
            me = y if cc == 0 else x
            arrive, leave = r2_copies(cc, v), t1_copies(cc, v)
            arrive[0].wait_recv()
            arrive[1].wait_recv()
            for i in range(4):
                block = gchip(cc, v, i)
                add_into(block, r2.at[v, 0, i], r2.at[v, 1, i])
            for copy in leave:
                copy.start()

        by_core(body)

    def rs_d(v):
        def body(cc):
            plus, minus = (xp, xm) if cc == 0 else (yp, ym)
            arrive, leave = t1_copies(cc, v), t2_copies(cc, v)
            arrive[0].wait_recv()
            add_into(gchip(cc, v, plus, TOP), t1.at[v, 0])
            leave[0].start()
            arrive[1].wait_recv()
            add_into(gchip(cc, v, minus, BOTTOM), t1.at[v, 1])
            leave[1].start()

        by_core(body)

    def rs_e(v):
        def body(cc):
            for copy in t2_copies(cc, v):
                copy.wait_recv()

        by_core(body)
        return (
            xs[4 * v + y, x].astype(F32) + t2[v, 0].astype(F32) + t2[v, 1].astype(F32)
        )

    v0, v1 = 1 - zl, zl
    weight_term(v0)
    rs_a(v0)
    weight_term(v1)
    rs_a(v1)
    rs_b(v0)
    rs_b(v1)
    rs_c(v0)
    rs_c(v1)
    rs_d(v0)
    rs_d(v1)
    xs[4 * v0 + y, x] = rs_e(v0).astype(BF16)
    pair = device(x, y, 2 * s + 1 - zl, c)
    cross = remote(xs.at[4 * v0 + y, x], z1, zsend, zrecv, pair)
    cross.start()
    sf[...] = rs_e(v1)
    cross.wait_recv()
    sf[...] = sf[...] + z1[...].astype(F32)
    last = remote(sf.at[sib_rows], o1, osend, orecv, sib)
    last.start()
    out_ref[:, mine] = sf[my_rows, :]
    last.wait_recv()
    out_ref[:, other] = o1[...]

    for copy in gives(1 - c, my_rows):
        copy.wait_send()
    for d in range(1, 8):
        raw(d).wait_send()

    @pl.loop(0, UNITS)
    def _(u):
        def body(cc):
            for copy in p_copies(wa, cc, u, u) + q_copies(wa, cc, u, u):
                copy.wait_send()
            for i in range(4):
                d_copy(wa, cc, u, u, i).wait_send()

        by_core(body)

    def own_sent(cc):
        for copy in p_copies(wz, cc, own, UNITS) + q_copies(wz, cc, own, UNITS):
            copy.wait_send()
        for i in range(4):
            d_copy(wz, cc, own, UNITS, i).wait_send()

    by_core(own_sent)
    for i in range(2):
        for r in range(1, 4):
            up(r, i).wait_send()
            down(r, i).wait_send()
        for slot in range(7):
            e_copy(slot, i).wait_send()
    up(4, 0).wait_send()
    down(4, 1).wait_send()
    last.wait_send()
    cross.wait_send()
    give_g.wait_send()
    normed_copy().wait_send()

    @pl.loop(0, 2)
    def _(v):
        def body(cc):
            for copies in (r1_copies, r2_copies, t1_copies, t2_copies):
                for copy in copies(cc, v):
                    copy.wait_send()

        by_core(body)


def local(inputs, weights, cotangents, lengths):
    rows = inputs.shape[0] * inputs.shape[1]
    dma = pltpu.SemaphoreType.DMA
    vmem = pl.BlockSpec(memory_space=pltpu.VMEM)
    out = pl.pallas_call(
        kernel,
        out_shape=jax.ShapeDtypeStruct((32, D), F32),
        in_specs=[
            pl.BlockSpec(memory_space=pl.ANY),
            vmem,
            vmem,
            pl.BlockSpec(memory_space=pltpu.SMEM),
        ],
        out_specs=vmem,
        scratch_shapes=[
            pltpu.VMEM((8, 2, 4, 4, 64, XY), BF16),
            pltpu.VMEM((8, 2, 4, 4, 64, Z), BF16),
            pltpu.VMEM((8, 4, 64, HALF), BF16),
            pltpu.VMEM((4, ROWS, D), F32),
            pltpu.VMEM((4, ROWS, 128), F32),
            pltpu.VMEM((ROWS, D), BF16),
            pltpu.VMEM((2, ROWS, D), BF16),
            pltpu.VMEM((2, ROWS, HALF), BF16),
            pltpu.VMEM((ROWS, D), BF16),
            pltpu.VMEM((ROWS, D), F32),
            pltpu.VMEM((2, 2, 2, 64, HALF), BF16),
            pltpu.VMEM((2, 2, 4, 64, HALF), BF16),
            pltpu.VMEM((2, 2, 32, HALF), BF16),
            pltpu.VMEM((2, 2, 64, HALF), BF16),
            pltpu.VMEM((64, HALF), BF16),
            pltpu.VMEM((64, HALF), F32),
            pltpu.VMEM((32, HALF), F32),
            dma((4,)),
            dma((2,)),
            dma((2,)),
            dma((7,)),
            dma((8,)),
            dma((4, 2)),
            dma((4, 2)),
            dma((4, 2)),
            dma((4, 2)),
            dma((7, 2)),
            dma((7, 2)),
            dma((9, 4)),
            dma((9, 4)),
            dma((9, 4)),
            dma((9, 4)),
            dma((9, 4)),
            dma((9, 4)),
            dma((2,)),
            dma((2,)),
            dma((2, 2)),
            dma((2, 2)),
            dma((2, 2)),
            dma((2, 2)),
            dma((2, 2)),
            dma((2, 2)),
            dma((2, 2)),
            dma((2, 2)),
            dma,
            dma,
            dma,
            dma,
        ],
        compiler_params=pltpu.CompilerParams(
            collective_id=0, has_side_effects=True, vmem_limit_bytes=63 * 2**20
        ),
        cost_estimate=pl.CostEstimate(
            flops=9 * 2 * ROWS * D * D, bytes_accessed=36 * 2**20, transcendentals=4 * ROWS * D
        ),
    )(inputs.reshape(4, rows // 4, D), weights[0], cotangents.reshape(rows, D), lengths)
    return out[None]


def solution(mesh):
    in_specs = (
        P(None, "fsdp", None),
        P("section", "fsdp", None),
        P(None, "fsdp", None),
        P(None, "fsdp"),
    )
    out_specs = P("section", "fsdp", None)
    return jax.shard_map(local, mesh=mesh, in_specs=in_specs, out_specs=out_specs, check_vma=False)
```

time: 174 us -> 161 us (0.925)
  the two profiles are of different devices: /device:TPU:161 before, /device:TPU:1 now
where the time goes in v2:
time: 161 us
  Pallas kernels  159 us (99%)
  local copies, waits for them, and re-layouts  1.67 us (1%)
    pallas_call x1, Pallas kernels, local(): pl.pallas_call(kernel, out_shape=jax.ShapeDtypeStruct((32, D), F32), in_s...  159 us

profile of v2, /device:TPU:1, one launch (start us, length us, event | category | flops | bytes accessed | tf_op | source)
XLA Modules:
  0.0 160.5 jit_solution(12064968410916189649)
XLA Ops:
  0.0 158.9 %shard_map.46 = f32[32,2048]{1,0:T(8,128)} custom-call(bf16[4,64,2048]{2,1,0:T(8,128)(2,1)} %bitcast.5, bf16[32,2048]{1,0:T(8,128)(2,1)} %bitcast.7, bf16[256,2048]{1,0:T(8,128)(2,1)} %bitcast.6, s32[2,2]{1,0:T(2,128)} %len_ref.1), custom_call_target="tpu_custom_call" | custom-call | flops 19327352832 | bytes 37748736 | tf_op jit(solution)/shard_map/pallas_call | solution.py:650
  158.9 1.7 %copy.6 = f32[1,32,2048]{2,1,0:T(8,128)} copy(f32[1,32,2048]{2,1,0:T(8,128)} %bitcast.4) | data formatting | bytes 524288

commit v3 on v2

--- a/solution.py
+++ b/solution.py
@@ -20,7 +20,7 @@
 XY = 768
 Z = HALF - XY
 UNITS = 8
-READY = ((4, 6, 8, 9), (6, 7, 8, 9), (6, 7, 8, 9), (6, 8, 9, 10))
+READY = ((3, 6, 7, 9), (6, 7, 8, 9), (7, 8, 9, 10), (6, 7, 9, 10))
 FIRST, SECOND = pl.ds(0, 2), pl.ds(2, 2)
 TOP, BOTTOM = pl.ds(0, 32), pl.ds(32, 32)
 
@@ -91,11 +91,6 @@
     ]
     for copy in in_w:
         copy.start()
-    for m in range(2):
-        for q in range(2):
-            rows = pl.ds(128 * m + 64 * q, 64)
-            live = lax.broadcasted_iota(jnp.int32, (64, D), 0) < len_ref[m, q]
-            gr[rows, :] = jnp.where(live, cot_ref[rows, :].astype(F32), 0.0).astype(BF16)
     pl.semaphore_wait(barrier, 12)
 
     def gives(core, rows):
@@ -113,7 +108,7 @@
 
     for copy in gives(1 - c, my_rows):
         copy.start()
-    for copy in in_x + in_w:
+    for copy in in_w:
         copy.wait()
     for copy in gives(c, sib_rows):
         copy.wait_recv()
@@ -160,21 +155,25 @@
         kh, uz = 2 * (u // 2) + cc, lax.rem(u, 2)
         me, plus, minus = (y, yp, ym) if cc == 0 else (x, xp, xm)
         to_plus, to_minus = (dyp, dym) if cc == 0 else (dxp, dxm)
-        own = row(w, cc, kh, uz, me)
+        first, second = row(w, cc, kh, uz, me, FIRST), row(w, cc, kh, uz, me, SECOND)
         from_minus, from_plus = row(w, cc, kh, uz, minus, FIRST), row(w, cc, kh, uz, plus, SECOND)
         return (
-            remote(own, own, qsend.at[b, 0], qrecv.at[b, 0], to_plus),
-            remote(own, own, qsend.at[b, 1], qrecv.at[b, 1], to_minus),
-            remote(from_minus, from_minus, qsend.at[b, 2], qrecv.at[b, 2], to_plus),
-            remote(from_plus, from_plus, qsend.at[b, 3], qrecv.at[b, 3], to_minus),
+            remote(first, first, qsend.at[b, 0], qrecv.at[b, 0], to_plus),
+            remote(second, second, qsend.at[b, 1], qrecv.at[b, 1], to_minus),
+            remote(second, second, qsend.at[b, 2], qrecv.at[b, 2], to_plus),
+            remote(first, first, qsend.at[b, 3], qrecv.at[b, 3], to_minus),
+            remote(from_minus, from_minus, qsend.at[b, 4], qrecv.at[b, 4], to_plus),
+            remote(from_plus, from_plus, qsend.at[b, 5], qrecv.at[b, 5], to_minus),
         )
 
     def q_landed(w, cc, u, b, i):
         kh, uz = 2 * (u // 2) + cc, lax.rem(u, 2)
         plus, minus, far = (yp, ym, y2) if cc == 0 else (xp, xm, x2)
         land = (
-            row(w, cc, kh, uz, minus),
-            row(w, cc, kh, uz, plus),
+            row(w, cc, kh, uz, minus, FIRST),
+            row(w, cc, kh, uz, plus, SECOND),
+            row(w, cc, kh, uz, minus, SECOND),
+            row(w, cc, kh, uz, plus, FIRST),
             row(w, cc, kh, uz, far, FIRST),
             row(w, cc, kh, uz, far, SECOND),
         )[i]
@@ -192,7 +191,8 @@
 
     def unit(t):
         rest = t - 2
-        rest = jnp.where(rest < 2 * s, rest, rest + 2)
+        near = jnp.where(rest < 2, rest + 2, jnp.where(rest < 4, rest - 2, rest + 2))
+        rest = jnp.where(s == 2, near, jnp.where(rest < 2 * s, rest, rest + 2))
         return jnp.where(t == 0, z, jnp.where(t == 1, 2 * s + 1 - zl, rest))
 
     def stage_p1(w, u, b):
@@ -222,8 +222,8 @@
             copies = q_copies(w, cc, u, b)
             p_landed(w, cc, u, b, 2)
             p_landed(w, cc, u, b, 3)
-            copies[0].start()
-            copies[1].start()
+            for copy in copies[:4]:
+                copy.start()
             d_copy(w, cc, u, b, 0).start()
 
         by_core(body)
@@ -232,18 +232,20 @@
         def body(cc):
             copies = q_copies(w, cc, u, b)
             q_landed(w, cc, u, b, 0)
-            copies[2].start()
+            copies[4].start()
             q_landed(w, cc, u, b, 1)
-            copies[3].start()
+            copies[5].start()
+
+        by_core(body)
+
+    def stage_f(w, u, b):
+        def body(cc):
+            q_landed(w, cc, u, b, 2)
             d_copy(w, cc, u, b, 1).start()
+            q_landed(w, cc, u, b, 3)
             d_copy(w, cc, u, b, 2).start()
-
-        by_core(body)
-
-    def stage_f(w, u, b):
-        def body(cc):
-            q_landed(w, cc, u, b, 2)
-            q_landed(w, cc, u, b, 3)
+            q_landed(w, cc, u, b, 4)
+            q_landed(w, cc, u, b, 5)
             d_copy(w, cc, u, b, 3).start()
 
         by_core(body)
@@ -366,6 +368,13 @@
     stage_p1(wa, own, own)
     for d in (1, 7, 2, 6, 3, 5, 4):
         raw(d).start()
+    for m in range(2):
+        for q in range(2):
+            rows = pl.ds(128 * m + 64 * q, 64)
+            live = lax.broadcasted_iota(jnp.int32, (64, D), 0) < len_ref[m, q]
+            gr[rows, :] = jnp.where(live, cot_ref[rows, :].astype(F32), 0.0).astype(BF16)
+    for copy in in_x:
+        copy.wait()
     stage_p2(wz, own, UNITS)
     stage_p2(wa, own, own)
     stage_q1(wz, own, UNITS)
@@ -374,11 +383,15 @@
     raw_landed(near)
     stage_p1(wa, near, near)
     stage_q2(wz, own, UNITS)
+    stage_p2(wa, near, near)
+    stage_q2(wa, own, own)
     stage_f(wz, own, UNITS)
-    for part_ in range(2):
-        up(1, part_).start()
-        down(1, part_).start()
-    stage_p2(wa, near, near)
+    for i in range(2):
+        up(1, i).start()
+        down(1, i).start()
+    third = unit(2)
+    raw_landed(third)
+    stage_p1(wa, third, third)
 
     @pl.loop(1, UNITS + 3)
     def _(i):
@@ -392,27 +405,27 @@
             raw_landed(u)
             stage_p1(w, u, b)
 
-        when_unit(1, first_stage)
         when_unit(0, stage_q1)
+        when_unit(2, first_stage)
         when_unit(1, stage_p2)
-        when_unit(-1, stage_q2)
-        when_unit(-2, stage_f)
-        pl.when(i == 1)(lambda: relay(1, 0))
-        pl.when(i == 2)(lambda: relay(1, 1))
-        pl.when(i == 3)(lambda: relay(2, 0))
-        pl.when(i == 4)(lambda: relay(2, 1))
-
-        @pl.when(i == 5)
-        def _():
-            relay(3, 0)
-            relay(3, 1)
-
-        pl.when(i == 6)(relay_end)
         k = -1
         for section in range(4):
             for number in range(4):
                 k = jnp.where((s == section) & (i == READY[section][number]), number, k)
         pl.when(k >= 0)(lambda: forward(jnp.maximum(k, 0)))
+        when_unit(0, stage_q2)
+        when_unit(-1, stage_f)
+        pl.when(i == 1)(lambda: relay(1, 0))
+        pl.when(i == 2)(lambda: relay(1, 1))
+        pl.when(i == 3)(lambda: relay(2, 0))
+        pl.when(i == 4)(lambda: relay(2, 1))
+
+        @pl.when(i == 5)
+        def _():
+            relay(3, 0)
+            relay(3, 1)
+
+        pl.when(i == 6)(relay_end)
 
     def grad_pre(k):
         @pl.loop(0, ROWS // 32)
@@ -688,8 +701,8 @@
             dma((7, 2)),
             dma((9, 4)),
             dma((9, 4)),
-            dma((9, 4)),
-            dma((9, 4)),
+            dma((9, 6)),
+            dma((9, 6)),
             dma((9, 4)),
             dma((9, 4)),
             dma((2,)),

time: 161 us -> 156 us (0.969)
  Pallas kernels: 159 us -> 153 us
    pallas_call x1, Pallas kernels: 159 us -> 153 us  [local(): pl.pallas_call(kernel, out_shape=jax.ShapeDtypeStruct((32, D), F32), in_s...]
where the time goes in v3:
time: 156 us; the launch traced here: 155 us
  Pallas kernels  153 us (98%)
  local copies, waits for them, and re-layouts  1.67 us (1%)
    pallas_call x1, Pallas kernels, local(): pl.pallas_call(kernel, out_shape=jax.ShapeDtypeStruct((32, D), F32), in_s...  153 us

profile of v3, /device:TPU:1, one launch (start us, length us, event | category | flops | bytes accessed | tf_op | source)
XLA Modules:
  0.0 154.8 jit_solution(12512959572425814659)
XLA Ops:
  0.0 153.1 %shard_map.46 = f32[32,2048]{1,0:T(8,128)} custom-call(bf16[4,64,2048]{2,1,0:T(8,128)(2,1)} %bitcast.5, bf16[32,2048]{1,0:T(8,128)(2,1)} %bitcast.7, bf16[256,2048]{1,0:T(8,128)(2,1)} %bitcast.6, s32[2,2]{1,0:T(2,128)} %len_ref.1), custom_call_target="tpu_custom_call" | custom-call | flops 19327352832 | bytes 37748736 | tf_op jit(solution)/shard_map/pallas_call | solution.py:663
  153.1 1.7 %copy.6 = f32[1,32,2048]{2,1,0:T(8,128)} copy(f32[1,32,2048]{2,1,0:T(8,128)} %bitcast.4) | data formatting | bytes 524288

commit v4 on v3

--- a/solution.py
+++ b/solution.py
@@ -60,7 +60,8 @@
     dyp, dym = device(x, yp, z, c), device(x, ym, z, c)
 
     barrier = pltpu.get_barrier_semaphore()
-    for partner in (dxp, dxm, dyp, dym, sib):
+    pair_other = device(x, y, 2 * s + 1 - zl, 1 - c)
+    for partner in (dxp, dxm, dyp, dym, sib, pair_other):
         pl.semaphore_signal(barrier, inc=1, device_id=partner, device_id_type=MESH)
     for d in range(1, 8):
         pl.semaphore_signal(
@@ -91,7 +92,7 @@
     ]
     for copy in in_w:
         copy.start()
-    pl.semaphore_wait(barrier, 12)
+    pl.semaphore_wait(barrier, 13)
 
     def gives(core, rows):
         kh = 2 * s + core
@@ -340,9 +341,13 @@
             nw[c] = gp[...]
             normed_copy().start()
 
-        def section_columns(w, h, first, width):
-            cols = part(h, first, width)
-            u = jnp.dot(gp[...], w.reshape(D, width), preferred_element_type=F32)
+        @pl.loop(0, 2)
+        def _(h):
+            cols = part(h, 0, HALF)
+            w = jnp.concatenate(
+                [wa[2 * k + h].reshape(D, XY), wz[2 * k + h].reshape(D, Z)], axis=1
+            )
+            u = jnp.dot(gp[...], w, preferred_element_type=F32)
             uu = u * u
             t = jnp.tanh((GELU_C * u) * (1.0 + GELU_A * uu))
             cdf = 0.5 * (1.0 + t)
@@ -353,15 +358,9 @@
             @pl.when(k < 3)
             def _():
                 nxt = jnp.minimum(k + 1, 3)
-                inside = pl.ds(first, width)
-                before = xs[2 * k + h, :, :, inside].reshape(ROWS, width)
+                before = xs[2 * k + h].reshape(ROWS, HALF)
                 after = (before.astype(F32) + u * cdf).astype(BF16)
-                xs[2 * nxt + h, :, :, inside] = after.reshape(4, 64, width)
-
-        @pl.loop(0, 2)
-        def _(h):
-            section_columns(wa[2 * k + h], h, 0, XY)
-            section_columns(wz[2 * k + h], h, XY, Z)
+                xs[2 * nxt + h] = after.reshape(4, 64, HALF)
 
     own = unit(0)
     stage_p1(wz, own, UNITS)
@@ -427,29 +426,28 @@
 
         pl.when(i == 6)(relay_end)
 
-    def grad_pre(k):
-        @pl.loop(0, ROWS // 32)
-        def _(i):
-            rows = pl.ds(pl.multiple_of(i * 32, 32), 32)
-            gp[rows, :] = (gr[rows, :].astype(F32) * gd[k, rows, :]).astype(BF16)
+    @pl.loop(0, ROWS // 32)
+    def _(i):
+        rows = pl.ds(pl.multiple_of(i * 32, 32), 32)
+        gp[rows, :] = (gr[rows, :].astype(F32) * gd[3, rows, :]).astype(BF16)
 
     @pl.loop(0, 3 - s)
     def _(step):
         k = 3 - step
-        grad_pre(k)
-
-        @pl.loop(0, 4)
+
+        @pl.loop(0, 2)
         def _(j):
-            total = None
-            for h in range(2):
-                for w, first, width in ((wa, 0, XY), (wz, XY, Z)):
-                    tile = w[2 * k + h, j // 2, pl.ds(lax.rem(j, 2) * 2, 2)].reshape(512, width)
-                    term = lax.dot_general(
-                        gp[:, h * HALF + first : h * HALF + first + width], tile,
-                        (((1,), (1,)), ((), ())), preferred_element_type=F32,
-                    )
-                    total = term if total is None else total + term
-            gn[:, pl.ds(pl.multiple_of(j * 512, 512), 512)] = total
+            tile = jnp.concatenate(
+                [
+                    w[2 * k + h, j].reshape(HALF, width)
+                    for h in range(2)
+                    for w, width in ((wa, XY), (wz, Z))
+                ],
+                axis=1,
+            )
+            gn[:, part(j, 0, HALF)] = lax.dot_general(
+                gp[...], tile, (((1,), (1,)), ((), ())), preferred_element_type=F32
+            )
 
         @pl.loop(0, ROWS // 32)
         def _(i):
@@ -458,11 +456,11 @@
             g = gn[rows, :]
             inv = iv[k, rows, :][:, :1]
             mean = jnp.mean(g * xf, axis=-1, keepdims=True)
-            gr[rows, :] = (
-                gr[rows, :].astype(F32) + inv * g - xf * (inv * inv * inv * mean)
-            ).astype(BF16)
-
-    grad_pre(s)
+            grad = gr[rows, :].astype(F32) + inv * g - xf * (inv * inv * inv * mean)
+            grad = grad.astype(BF16)
+            gr[rows, :] = grad
+            gp[rows, :] = (grad.astype(F32) * gd[k - 1, rows, :]).astype(BF16)
+
     gw[c] = gp[:, mine]
     give_g = remote(gp.at[:, other], gw.at[c], nsend.at[1], nrecv.at[1], sib)
     give_g.start()
@@ -599,17 +597,21 @@
     rs_d(v0)
     rs_d(v1)
     xs[4 * v0 + y, x] = rs_e(v0).astype(BF16)
-    pair = device(x, y, 2 * s + 1 - zl, c)
-    cross = remote(xs.at[4 * v0 + y, x], z1, zsend, zrecv, pair)
-    cross.start()
+    def cross(core):
+        rows = pl.ds(pl.multiple_of(core * 32, 32), 32)
+        dest = device(x, y, 2 * s + 1 - zl, core)
+        return remote(xs.at[4 * v0 + y, x, rows], z1.at[c], zsend.at[core], zrecv.at[c], dest)
+
+    cross(0).start()
+    cross(1).start()
     sf[...] = rs_e(v1)
-    cross.wait_recv()
-    sf[...] = sf[...] + z1[...].astype(F32)
     last = remote(sf.at[sib_rows], o1, osend, orecv, sib)
     last.start()
-    out_ref[:, mine] = sf[my_rows, :]
+    for core in range(2):
+        remote(z1.at[core], z1.at[core], zsend.at[core], zrecv.at[core], sib).wait_recv()
+    out_ref[:, mine] = sf[my_rows, :] + z1[c].astype(F32)
     last.wait_recv()
-    out_ref[:, other] = o1[...]
+    out_ref[:, other] = o1[...] + z1[1 - c].astype(F32)
 
     for copy in gives(1 - c, my_rows):
         copy.wait_send()
@@ -642,7 +644,8 @@
     up(4, 0).wait_send()
     down(4, 1).wait_send()
     last.wait_send()
-    cross.wait_send()
+    cross(0).wait_send()
+    cross(1).wait_send()
     give_g.wait_send()
     normed_copy().wait_send()
 
@@ -685,7 +688,7 @@
             pltpu.VMEM((2, 2, 4, 64, HALF), BF16),
             pltpu.VMEM((2, 2, 32, HALF), BF16),
             pltpu.VMEM((2, 2, 64, HALF), BF16),
-            pltpu.VMEM((64, HALF), BF16),
+            pltpu.VMEM((2, 32, HALF), BF16),
             pltpu.VMEM((64, HALF), F32),
             pltpu.VMEM((32, HALF), F32),
             dma((4,)),
@@ -715,8 +718,8 @@
             dma((2, 2)),
             dma((2, 2)),
             dma((2, 2)),
-            dma,
-            dma,
+            dma((2,)),
+            dma((2,)),
             dma,
             dma,
         ],

time: 156 us -> 150 us (0.962)
  Pallas kernels: 153 us -> 149 us
    pallas_call x1, Pallas kernels: 153 us -> 149 us  [local(): pl.pallas_call(kernel, out_shape=jax.ShapeDtypeStruct((32, D), F32), in_s...]
where the time goes in v4:
time: 150 us
  Pallas kernels  149 us (99%)
  local copies, waits for them, and re-layouts  1.67 us (1%)
    pallas_call x1, Pallas kernels, local(): pl.pallas_call(kernel, out_shape=jax.ShapeDtypeStruct((32, D), F32), in_s...  149 us

profile of v4, /device:TPU:1, one launch (start us, length us, event | category | flops | bytes accessed | tf_op | source)
XLA Modules:
  0.0 150.2 jit_solution(3233598319802067714)
XLA Ops:
  0.0 148.5 %shard_map.46 = f32[32,2048]{1,0:T(8,128)} custom-call(bf16[4,64,2048]{2,1,0:T(8,128)(2,1)} %bitcast.5, bf16[32,2048]{1,0:T(8,128)(2,1)} %bitcast.7, bf16[256,2048]{1,0:T(8,128)(2,1)} %bitcast.6, s32[2,2]{1,0:T(2,128)} %len_ref.1), custom_call_target="tpu_custom_call" | custom-call | flops 19327352832 | bytes 37748736 | tf_op jit(solution)/shard_map/pallas_call | solution.py:666
  148.5 1.7 %copy.6 = f32[1,32,2048]{2,1,0:T(8,128)} copy(f32[1,32,2048]{2,1,0:T(8,128)} %bitcast.4) | data formatting | bytes 524288

commit v5 on v4

--- a/solution.py
+++ b/solution.py
@@ -20,7 +20,7 @@
 XY = 768
 Z = HALF - XY
 UNITS = 8
-READY = ((3, 6, 7, 9), (6, 7, 8, 9), (7, 8, 9, 10), (6, 7, 9, 10))
+READY = ((4, 6, 8, 10), (6, 7, 8, 10), (8, 9, 10, 11), (6, 8, 10, 11))
 FIRST, SECOND = pl.ds(0, 2), pl.ds(2, 2)
 TOP, BOTTOM = pl.ds(0, 32), pl.ds(32, 32)
 
@@ -180,6 +180,31 @@
         )[i]
         remote(land, land, qsend.at[b, i], qrecv.at[b, i], sib).wait_recv()
 
+    def o_block(w, cc, ahead, off):
+        qs = ((y, yp, y2, ym) if cc == 0 else (x, xp, x2, xm))[ahead]
+        ps = ((x, xp, x2, xm) if cc == 0 else (y, yp, y2, ym))[off]
+        at = (qs, ps) if cc == 0 else (ps, qs)
+        return w.at[(2 * s + cc, zl) + at]
+
+    def o_copies(w, cc, b):
+        plus, minus = (dyp, dym) if cc == 0 else (dxp, dxm)
+        moves = [(0, off, way) for off in (0, -1, 1, 2) for way in (True, False)]
+        moves += [(-1, 0, True), (1, -1, False), (1, 1, False), (-1, 2, True)]
+        copies = []
+        for i, (ahead, off, way) in enumerate(moves):
+            block = o_block(w, cc, ahead, off)
+            copies.append(
+                remote(block, block, qsend.at[b, i], qrecv.at[b, i], plus if way else minus)
+            )
+        return copies
+
+    def o_landed(w, cc, b, *which):
+        lands = [(-1 if way else 1, off) for off in (0, -1, 1, 2) for way in (True, False)]
+        lands += [(2, 0), (2, -1), (2, 1), (2, 2)]
+        for i in which:
+            block = o_block(w, cc, *lands[i])
+            remote(block, block, qsend.at[b, i], qrecv.at[b, i], sib).wait_recv()
+
     def d_copy(w, cc, u, b, i):
         kh, uz = 2 * (u // 2) + cc, lax.rem(u, 2)
         at = ((y, ym, yp, y2) if cc == 0 else (x, xm, xp, x2))[i]
@@ -248,6 +273,68 @@
             q_landed(w, cc, u, b, 4)
             q_landed(w, cc, u, b, 5)
             d_copy(w, cc, u, b, 3).start()
+
+        by_core(body)
+
+    def own_0(w, b):
+        def body(cc):
+            for copy in p_copies(w, cc, z, b)[:2] + tuple(o_copies(w, cc, b)[:2]):
+                copy.start()
+
+        by_core(body)
+
+    def own_1(w, b):
+        def body(cc):
+            first, row_ = p_copies(w, cc, z, b), o_copies(w, cc, b)
+            p_landed(w, cc, z, b, 0)
+            first[2].start()
+            row_[2].start()
+            row_[3].start()
+            p_landed(w, cc, z, b, 1)
+            first[3].start()
+            row_[4].start()
+            row_[5].start()
+
+        by_core(body)
+
+    def own_2(w, b):
+        def body(cc):
+            row_ = o_copies(w, cc, b)
+            p_landed(w, cc, z, b, 2)
+            p_landed(w, cc, z, b, 3)
+            row_[6].start()
+            row_[7].start()
+            d_copy(w, cc, z, b, 0).start()
+
+        by_core(body)
+
+    def own_3(w, b):
+        def body(cc):
+            row_ = o_copies(w, cc, b)
+            o_landed(w, cc, b, 0)
+            row_[8].start()
+            o_landed(w, cc, b, 3)
+            row_[9].start()
+            o_landed(w, cc, b, 5)
+            row_[10].start()
+
+        by_core(body)
+
+    def own_4(w, b):
+        def body(cc):
+            o_landed(w, cc, b, 6)
+            o_copies(w, cc, b)[11].start()
+            o_landed(w, cc, b, 2, 4)
+            d_copy(w, cc, z, b, 1).start()
+            o_landed(w, cc, b, 1, 7)
+            d_copy(w, cc, z, b, 2).start()
+
+        by_core(body)
+
+    def own_5(w, b):
+        def body(cc):
+            o_landed(w, cc, b, 8, 9, 10, 11)
+            d_copy(w, cc, z, b, 3).start()
 
         by_core(body)
 
@@ -362,9 +449,8 @@
                 after = (before.astype(F32) + u * cdf).astype(BF16)
                 xs[2 * nxt + h] = after.reshape(4, 64, HALF)
 
-    own = unit(0)
-    stage_p1(wz, own, UNITS)
-    stage_p1(wa, own, own)
+    own_0(wz, UNITS)
+    own_0(wa, z)
     for d in (1, 7, 2, 6, 3, 5, 4):
         raw(d).start()
     for m in range(2):
@@ -374,17 +460,18 @@
             gr[rows, :] = jnp.where(live, cot_ref[rows, :].astype(F32), 0.0).astype(BF16)
     for copy in in_x:
         copy.wait()
-    stage_p2(wz, own, UNITS)
-    stage_p2(wa, own, own)
-    stage_q1(wz, own, UNITS)
-    stage_q1(wa, own, own)
+    own_1(wz, UNITS)
+    own_1(wa, z)
+    own_2(wz, UNITS)
     near = unit(1)
     raw_landed(near)
     stage_p1(wa, near, near)
-    stage_q2(wz, own, UNITS)
+    own_2(wa, z)
+    own_3(wz, UNITS)
     stage_p2(wa, near, near)
-    stage_q2(wa, own, own)
-    stage_f(wz, own, UNITS)
+    own_3(wa, z)
+    own_4(wz, UNITS)
+    own_5(wz, UNITS)
     for i in range(2):
         up(1, i).start()
         down(1, i).start()
@@ -392,10 +479,10 @@
     raw_landed(third)
     stage_p1(wa, third, third)
 
-    @pl.loop(1, UNITS + 3)
+    @pl.loop(1, UNITS + 4)
     def _(i):
         def when_unit(ahead, stage):
-            @pl.when((i + ahead >= 0) & (i + ahead < UNITS))
+            @pl.when((i + ahead >= 1) & (i + ahead < UNITS))
             def _():
                 u = unit(i + ahead)
                 stage(wa, u, u)
@@ -404,19 +491,29 @@
             raw_landed(u)
             stage_p1(w, u, b)
 
-        when_unit(0, stage_q1)
         when_unit(2, first_stage)
         when_unit(1, stage_p2)
+        when_unit(0, stage_q1)
         k = -1
         for section in range(4):
             for number in range(4):
                 k = jnp.where((s == section) & (i == READY[section][number]), number, k)
         pl.when(k >= 0)(lambda: forward(jnp.maximum(k, 0)))
-        when_unit(0, stage_q2)
-        when_unit(-1, stage_f)
-        pl.when(i == 1)(lambda: relay(1, 0))
-        pl.when(i == 2)(lambda: relay(1, 1))
-        pl.when(i == 3)(lambda: relay(2, 0))
+        when_unit(-1, stage_q2)
+        when_unit(-2, stage_f)
+
+        @pl.when(i == 1)
+        def _():
+            own_4(wa, z)
+            own_5(wa, z)
+
+        pl.when(i == 2)(lambda: relay(1, 0))
+
+        @pl.when(i == 3)
+        def _():
+            relay(1, 1)
+            relay(2, 0)
+
         pl.when(i == 4)(lambda: relay(2, 1))
 
         @pl.when(i == 5)
@@ -621,18 +718,25 @@
     @pl.loop(0, UNITS)
     def _(u):
         def body(cc):
-            for copy in p_copies(wa, cc, u, u) + q_copies(wa, cc, u, u):
+            for copy in p_copies(wa, cc, u, u):
                 copy.wait_send()
             for i in range(4):
                 d_copy(wa, cc, u, u, i).wait_send()
 
+            @pl.when(u != z)
+            def _():
+                for copy in q_copies(wa, cc, u, u):
+                    copy.wait_send()
+
         by_core(body)
 
     def own_sent(cc):
-        for copy in p_copies(wz, cc, own, UNITS) + q_copies(wz, cc, own, UNITS):
+        for copy in p_copies(wz, cc, z, UNITS):
+            copy.wait_send()
+        for copy in o_copies(wz, cc, UNITS) + o_copies(wa, cc, z):
             copy.wait_send()
         for i in range(4):
-            d_copy(wz, cc, own, UNITS, i).wait_send()
+            d_copy(wz, cc, z, UNITS, i).wait_send()
 
     by_core(own_sent)
     for i in range(2):
@@ -704,8 +808,8 @@
             dma((7, 2)),
             dma((9, 4)),
             dma((9, 4)),
-            dma((9, 6)),
-            dma((9, 6)),
+            dma((9, 12)),
+            dma((9, 12)),
             dma((9, 4)),
             dma((9, 4)),
             dma((2,)),

time: 150 us -> 153 us (1.020)
  Pallas kernels: 149 us -> 151 us
    pallas_call x1, Pallas kernels: 149 us -> 151 us  [local(): pl.pallas_call(kernel, out_shape=jax.ShapeDtypeStruct((32, D), F32), in_s...]
where the time goes in v5:
time: 153 us; the launch traced here: 152 us
  Pallas kernels  151 us (99%)
  local copies, waits for them, and re-layouts  1.67 us (1%)
    pallas_call x1, Pallas kernels, local(): pl.pallas_call(kernel, out_shape=jax.ShapeDtypeStruct((32, D), F32), in_s...  151 us

profile of v5, /device:TPU:1, one launch (start us, length us, event | category | flops | bytes accessed | tf_op | source)
XLA Modules:
  0.0 152.4 jit_solution(268871948444141780)
XLA Ops:
  0.0 150.7 %shard_map.46 = f32[32,2048]{1,0:T(8,128)} custom-call(bf16[4,64,2048]{2,1,0:T(8,128)(2,1)} %bitcast.5, bf16[32,2048]{1,0:T(8,128)(2,1)} %bitcast.7, bf16[256,2048]{1,0:T(8,128)(2,1)} %bitcast.6, s32[2,2]{1,0:T(2,128)} %len_ref.1), custom_call_target="tpu_custom_call" | custom-call | flops 19327352832 | bytes 37748736 | tf_op jit(solution)/shard_map/pallas_call | solution.py:770
  150.7 1.7 %copy.6 = f32[1,32,2048]{2,1,0:T(8,128)} copy(f32[1,32,2048]{2,1,0:T(8,128)} %bitcast.4) | data formatting | bytes 524288

commit v6 on v5

--- a/solution.py
+++ b/solution.py
@@ -20,7 +20,7 @@
 XY = 768
 Z = HALF - XY
 UNITS = 8
-READY = ((4, 6, 8, 10), (6, 7, 8, 10), (8, 9, 10, 11), (6, 8, 10, 11))
+READY = ((4, 6, 7, 9), (6, 7, 8, 9), (7, 8, 9, 10), (6, 7, 9, 10))
 FIRST, SECOND = pl.ds(0, 2), pl.ds(2, 2)
 TOP, BOTTOM = pl.ds(0, 32), pl.ds(32, 32)
 
@@ -451,8 +451,8 @@
 
     own_0(wz, UNITS)
     own_0(wa, z)
-    for d in (1, 7, 2, 6, 3, 5, 4):
-        raw(d).start()
+    raw(1).start()
+    raw(7).start()
     for m in range(2):
         for q in range(2):
             rows = pl.ds(128 * m + 64 * q, 64)
@@ -462,16 +462,21 @@
         copy.wait()
     own_1(wz, UNITS)
     own_1(wa, z)
+    raw(2).start()
+    raw(6).start()
     own_2(wz, UNITS)
     near = unit(1)
     raw_landed(near)
     stage_p1(wa, near, near)
     own_2(wa, z)
+    raw(3).start()
+    raw(5).start()
     own_3(wz, UNITS)
     stage_p2(wa, near, near)
     own_3(wa, z)
     own_4(wz, UNITS)
     own_5(wz, UNITS)
+    raw(4).start()
     for i in range(2):
         up(1, i).start()
         down(1, i).start()
@@ -479,7 +484,7 @@
     raw_landed(third)
     stage_p1(wa, third, third)
 
-    @pl.loop(1, UNITS + 4)
+    @pl.loop(1, UNITS + 3)
     def _(i):
         def when_unit(ahead, stage):
             @pl.when((i + ahead >= 1) & (i + ahead < UNITS))
@@ -491,16 +496,16 @@
             raw_landed(u)
             stage_p1(w, u, b)
 
+        when_unit(0, stage_q1)
         when_unit(2, first_stage)
         when_unit(1, stage_p2)
-        when_unit(0, stage_q1)
         k = -1
         for section in range(4):
             for number in range(4):
                 k = jnp.where((s == section) & (i == READY[section][number]), number, k)
         pl.when(k >= 0)(lambda: forward(jnp.maximum(k, 0)))
-        when_unit(-1, stage_q2)
-        when_unit(-2, stage_f)
+        when_unit(0, stage_q2)
+        when_unit(-1, stage_f)
 
         @pl.when(i == 1)
         def _():
@@ -514,13 +519,12 @@
             relay(1, 1)
             relay(2, 0)
 
-        pl.when(i == 4)(lambda: relay(2, 1))
-
-        @pl.when(i == 5)
+        @pl.when(i == 4)
         def _():
+            relay(2, 1)
             relay(3, 0)
-            relay(3, 1)
-
+
+        pl.when(i == 5)(lambda: relay(3, 1))
         pl.when(i == 6)(relay_end)
 
     @pl.loop(0, ROWS // 32)

time: 153 us -> 155 us (1.013)
  Pallas kernels: 151 us -> 153 us
    pallas_call x1, Pallas kernels: 151 us -> 153 us  [local(): pl.pallas_call(kernel, out_shape=jax.ShapeDtypeStruct((32, D), F32), in_s...]
where the time goes in v6:
time: 155 us
  Pallas kernels  153 us (99%)
  local copies, waits for them, and re-layouts  1.67 us (1%)
    pallas_call x1, Pallas kernels, local(): pl.pallas_call(kernel, out_shape=jax.ShapeDtypeStruct((32, D), F32), in_s...  153 us

profile of v6, /device:TPU:1, one launch (start us, length us, event | category | flops | bytes accessed | tf_op | source)
XLA Modules:
  0.0 154.6 jit_solution(11876078463912098287)
XLA Ops:
  0.0 152.9 %shard_map.46 = f32[32,2048]{1,0:T(8,128)} custom-call(bf16[4,64,2048]{2,1,0:T(8,128)(2,1)} %bitcast.5, bf16[32,2048]{1,0:T(8,128)(2,1)} %bitcast.7, bf16[256,2048]{1,0:T(8,128)(2,1)} %bitcast.6, s32[2,2]{1,0:T(2,128)} %len_ref.1), custom_call_target="tpu_custom_call" | custom-call | flops 19327352832 | bytes 37748736 | tf_op jit(solution)/shard_map/pallas_call | solution.py:774
  152.9 1.7 %copy.6 = f32[1,32,2048]{2,1,0:T(8,128)} copy(f32[1,32,2048]{2,1,0:T(8,128)} %bitcast.4) | data formatting | bytes 524288

commit v7 on v4

--- a/solution.py
+++ b/solution.py
@@ -47,8 +47,9 @@
 def kernel(
     x_ref, w_ref, cot_ref, len_ref, out_ref,
     wa, wz, xs, gd, iv, gp, nw, gw, gr, gn, r1, r2, t1, t2, z1, sf, o1,
-    loc, xsend, xrecv, rsend, rrecv, usend, urecv, lsend, lrecv, esend, erecv, psend, precv, qsend, qrecv, dsend, drecv,
-    nsend, nrecv, r1s, r1r, r2s, r2r, t1s, t1r, t2s, t2r, zsend, zrecv, osend, orecv,
+    lens, loc, xsend, xrecv, rsend, rrecv, usend, urecv, lsend, lrecv, esend, erecv,
+    psend, precv, qsend, qrecv, dsend, drecv,
+    nsend, nrecv, gsend, r1r, r2r, t1r, t2r, zsend, zrecv, osend, orecv,
 ):
     s, zl, x, y, c = position()
     z = 2 * s + zl
@@ -60,13 +61,10 @@
     dyp, dym = device(x, yp, z, c), device(x, ym, z, c)
 
     barrier = pltpu.get_barrier_semaphore()
+    above, below = device(x, y, lax.rem(z + 1, 8), c), device(x, y, lax.rem(z + 7, 8), c)
     pair_other = device(x, y, 2 * s + 1 - zl, 1 - c)
-    for partner in (dxp, dxm, dyp, dym, sib, pair_other):
+    for partner in (dxp, dxm, dyp, dym, above, below, sib, pair_other):
         pl.semaphore_signal(barrier, inc=1, device_id=partner, device_id_type=MESH)
-    for d in range(1, 8):
-        pl.semaphore_signal(
-            barrier, inc=1, device_id=device(x, y, lax.rem(z + d, 8), c), device_id_type=MESH
-        )
 
     def part(core, first, width):
         return pl.ds(pl.multiple_of(core * HALF + first, 256), width)
@@ -75,6 +73,8 @@
         pltpu.make_async_copy(x_ref.at[:, :, h * HALF : (h + 1) * HALF], xs.at[h], loc.at[3 * h])
         for h in range(2)
     ]
+    in_x.append(pltpu.make_async_copy(cot_ref, gr, loc.at[4]))
+    in_x.append(pltpu.make_async_copy(len_ref, lens, loc.at[5]))
     for copy in in_x:
         copy.start()
     mine = pl.ds(pl.multiple_of(c * HALF, HALF), HALF)
@@ -92,7 +92,7 @@
     ]
     for copy in in_w:
         copy.start()
-    pl.semaphore_wait(barrier, 13)
+    pl.semaphore_wait(barrier, 8)
 
     def gives(core, rows):
         kh = 2 * s + core
@@ -114,10 +114,29 @@
     for copy in gives(c, sib_rows):
         copy.wait_recv()
 
-    def raw(d):
-        block = wa.at[2 * s + c, zl, y, x]
-        dest = device(x, y, lax.rem(z + d, 8), c)
-        return remote(block, block, rsend.at[d - 1], rrecv.at[z], dest)
+    def raw_block(d, half=None):
+        v = lax.rem(z + 8 + d, 8)
+        at = (2 * (v // 2) + c, lax.rem(v, 2), y, x)
+        return wa.at[at] if half is None else wa.at[at + (half,)]
+
+    def raw_up(r, half=None):
+        block = raw_block(1 - r, half)
+        return remote(block, block, rsend.at[0], rrecv.at[0, r - 1], above)
+
+    def raw_down(r, half=None):
+        block = raw_block(r - 1, half)
+        return remote(block, block, rsend.at[1], rrecv.at[1, r - 1], below)
+
+    def raw_landed(r):
+        ups, downs = raw_block(-r, TOP if r == 4 else None), raw_block(r, BOTTOM if r == 4 else None)
+        remote(ups, ups, rsend.at[0], rrecv.at[0, r - 1], above).wait_recv()
+        remote(downs, downs, rsend.at[1], rrecv.at[1, r - 1], below).wait_recv()
+
+    def raw_step(r):
+        if r > 1:
+            raw_landed(r - 1)
+        raw_up(r, TOP if r == 4 else None).start()
+        raw_down(r, BOTTOM if r == 4 else None).start()
 
     def row(w, cc, kh, uz, i, part=None):
         if cc == 0:
@@ -129,16 +148,17 @@
         return w.at[at] if part is None else w.at[at + (part,)]
 
     def p_copies(w, cc, u, b):
+        fam = 0 if w is wa else 1
         kh, uz = 2 * (u // 2) + cc, lax.rem(u, 2)
         me, plus, minus = (x, xp, xm) if cc == 0 else (y, yp, ym)
         to_plus, to_minus = (dxp, dxm) if cc == 0 else (dyp, dym)
         own = chip(w, cc, kh, uz, me)
         from_minus, from_plus = chip(w, cc, kh, uz, minus, TOP), chip(w, cc, kh, uz, plus, BOTTOM)
         return (
-            remote(own, own, psend.at[b, 0], precv.at[b, 0], to_plus),
-            remote(own, own, psend.at[b, 1], precv.at[b, 1], to_minus),
-            remote(from_minus, from_minus, psend.at[b, 2], precv.at[b, 2], to_plus),
-            remote(from_plus, from_plus, psend.at[b, 3], precv.at[b, 3], to_minus),
+            remote(own, own, psend.at[fam], precv.at[b, 0], to_plus),
+            remote(own, own, psend.at[fam], precv.at[b, 1], to_minus),
+            remote(from_minus, from_minus, psend.at[fam], precv.at[b, 2], to_plus),
+            remote(from_plus, from_plus, psend.at[fam], precv.at[b, 2], to_minus),
         )
 
     def p_landed(w, cc, u, b, i):
@@ -147,24 +167,24 @@
         land = (
             chip(w, cc, kh, uz, minus),
             chip(w, cc, kh, uz, plus),
-            chip(w, cc, kh, uz, far, TOP),
-            chip(w, cc, kh, uz, far, BOTTOM),
+            chip(w, cc, kh, uz, far),
         )[i]
-        remote(land, land, psend.at[b, i], precv.at[b, i], sib).wait_recv()
+        remote(land, land, psend.at[0], precv.at[b, i], sib).wait_recv()
 
     def q_copies(w, cc, u, b):
+        fam = 0 if w is wa else 1
         kh, uz = 2 * (u // 2) + cc, lax.rem(u, 2)
         me, plus, minus = (y, yp, ym) if cc == 0 else (x, xp, xm)
         to_plus, to_minus = (dyp, dym) if cc == 0 else (dxp, dxm)
         first, second = row(w, cc, kh, uz, me, FIRST), row(w, cc, kh, uz, me, SECOND)
         from_minus, from_plus = row(w, cc, kh, uz, minus, FIRST), row(w, cc, kh, uz, plus, SECOND)
         return (
-            remote(first, first, qsend.at[b, 0], qrecv.at[b, 0], to_plus),
-            remote(second, second, qsend.at[b, 1], qrecv.at[b, 1], to_minus),
-            remote(second, second, qsend.at[b, 2], qrecv.at[b, 2], to_plus),
-            remote(first, first, qsend.at[b, 3], qrecv.at[b, 3], to_minus),
-            remote(from_minus, from_minus, qsend.at[b, 4], qrecv.at[b, 4], to_plus),
-            remote(from_plus, from_plus, qsend.at[b, 5], qrecv.at[b, 5], to_minus),
+            remote(first, first, qsend.at[fam], qrecv.at[b, 0], to_plus),
+            remote(second, second, qsend.at[fam], qrecv.at[b, 1], to_minus),
+            remote(second, second, qsend.at[fam], qrecv.at[b, 2], to_plus),
+            remote(first, first, qsend.at[fam], qrecv.at[b, 2], to_minus),
+            remote(from_minus, from_minus, qsend.at[fam], qrecv.at[b, 3], to_plus),
+            remote(from_plus, from_plus, qsend.at[fam], qrecv.at[b, 3], to_minus),
         )
 
     def q_landed(w, cc, u, b, i):
@@ -173,18 +193,16 @@
         land = (
             row(w, cc, kh, uz, minus, FIRST),
             row(w, cc, kh, uz, plus, SECOND),
-            row(w, cc, kh, uz, minus, SECOND),
-            row(w, cc, kh, uz, plus, FIRST),
-            row(w, cc, kh, uz, far, FIRST),
-            row(w, cc, kh, uz, far, SECOND),
+            row(w, cc, kh, uz, far),
+            row(w, cc, kh, uz, far),
         )[i]
-        remote(land, land, qsend.at[b, i], qrecv.at[b, i], sib).wait_recv()
+        remote(land, land, qsend.at[0], qrecv.at[b, i], sib).wait_recv()
 
     def d_copy(w, cc, u, b, i):
         kh, uz = 2 * (u // 2) + cc, lax.rem(u, 2)
         at = ((y, ym, yp, y2) if cc == 0 else (x, xm, xp, x2))[i]
         block = row(w, cc, kh, uz, at)
-        return remote(block, block, dsend.at[b, i], drecv.at[b, i], sib)
+        return remote(block, block, dsend.at[0 if w is wa else 1], drecv.at[b], sib)
 
     def by_core(body):
         for cc in (0, 1):
@@ -204,10 +222,6 @@
 
         by_core(body)
 
-    def raw_landed(u):
-        block = wa.at[2 * (u // 2) + c, lax.rem(u, 2), y, x]
-        remote(block, block, rsend.at[0], rrecv.at[u], sib).wait_recv()
-
     def stage_p2(w, u, b):
         def body(cc):
             copies = p_copies(w, cc, u, b)
@@ -222,7 +236,6 @@
         def body(cc):
             copies = q_copies(w, cc, u, b)
             p_landed(w, cc, u, b, 2)
-            p_landed(w, cc, u, b, 3)
             for copy in copies[:4]:
                 copy.start()
             d_copy(w, cc, u, b, 0).start()
@@ -243,17 +256,13 @@
         def body(cc):
             q_landed(w, cc, u, b, 2)
             d_copy(w, cc, u, b, 1).start()
+            d_copy(w, cc, u, b, 2).start()
             q_landed(w, cc, u, b, 3)
-            d_copy(w, cc, u, b, 2).start()
-            q_landed(w, cc, u, b, 4)
-            q_landed(w, cc, u, b, 5)
             d_copy(w, cc, u, b, 3).start()
 
         by_core(body)
 
     PARTS = (pl.ds(0, 2), pl.ds(2, 2))
-    above, below = device(x, y, lax.rem(z + 1, 8), c), device(x, y, lax.rem(z + 7, 8), c)
-
     def plane(d, part, core=None):
         v = lax.rem(z + 8 + d, 8)
         core = c if core is None else core
@@ -261,24 +270,24 @@
 
     def up(r, part):
         block = plane(1 - r, part)
-        return remote(block, block, usend.at[r - 1, part], urecv.at[r - 1, part], above)
+        return remote(block, block, usend, urecv.at[r - 1, part], above)
 
     def down(r, part):
         block = plane(r - 1, part)
-        return remote(block, block, lsend.at[r - 1, part], lrecv.at[r - 1, part], below)
+        return remote(block, block, lsend, lrecv.at[r - 1, part], below)
 
     def up_landed(r, part):
         block = plane(-r, part)
-        remote(block, block, usend.at[r - 1, part], urecv.at[r - 1, part], above).wait_recv()
+        remote(block, block, usend, urecv.at[r - 1, part], above).wait_recv()
 
     def down_landed(r, part):
         block = plane(r, part)
-        remote(block, block, lsend.at[r - 1, part], lrecv.at[r - 1, part], below).wait_recv()
+        remote(block, block, lsend, lrecv.at[r - 1, part], below).wait_recv()
 
     def e_copy(slot, part):
         d = (-1, -2, -3, 1, 2, 3, 4)[slot]
         block = plane(d, part)
-        return remote(block, block, esend.at[slot, part], erecv.at[slot, part], sib)
+        return remote(block, block, esend, erecv.at[slot], sib)
 
     def relay(r, part):
         up_landed(r, part)
@@ -309,24 +318,19 @@
         def _(uz):
             u = 2 * k + uz
 
-            def body(cc):
-                for i in range(4):
-                    d_copy(wa, 1 - cc, u, u, i).wait_recv()
-
-                @pl.when(u == z)
-                def _():
-                    for i in range(4):
-                        d_copy(wz, 1 - cc, u, UNITS, i).wait_recv()
-
-            by_core(body)
+            block = wa.at[2 * k + 1 - c, uz]
+            remote(block, block, dsend.at[0], drecv.at[u], sib).wait_recv()
+            z_block = wz.at[2 * k + 1 - c, uz]
+
+            @pl.when(u == z)
+            def _():
+                remote(z_block, z_block, dsend.at[1], drecv.at[UNITS], sib).wait_recv()
 
             @pl.when(u != z)
             def _():
                 d = lax.rem(u - z + 8, 8)
                 slot = jnp.where(d < 4, 2 + d, jnp.where(d == 4, 6, 7 - d))
-                for i in range(2):
-                    block = wz.at[2 * k + 1 - c, uz, PARTS[i]]
-                    remote(block, block, esend.at[slot, i], erecv.at[slot, i], sib).wait_recv()
+                remote(z_block, z_block, esend, erecv.at[slot], sib).wait_recv()
 
         @pl.loop(0, ROWS // 32)
         def _(i):
@@ -365,22 +369,22 @@
     own = unit(0)
     stage_p1(wz, own, UNITS)
     stage_p1(wa, own, own)
-    for d in (1, 7, 2, 6, 3, 5, 4):
-        raw(d).start()
+    raw_step(1)
+    stage_p2(wz, own, UNITS)
+    stage_p2(wa, own, own)
+    raw_step(2)
+    stage_q1(wz, own, UNITS)
+    stage_q1(wa, own, own)
+    for copy in in_x:
+        copy.wait()
     for m in range(2):
         for q in range(2):
             rows = pl.ds(128 * m + 64 * q, 64)
-            live = lax.broadcasted_iota(jnp.int32, (64, D), 0) < len_ref[m, q]
-            gr[rows, :] = jnp.where(live, cot_ref[rows, :].astype(F32), 0.0).astype(BF16)
-    for copy in in_x:
-        copy.wait()
-    stage_p2(wz, own, UNITS)
-    stage_p2(wa, own, own)
-    stage_q1(wz, own, UNITS)
-    stage_q1(wa, own, own)
+            live = lax.broadcasted_iota(jnp.int32, (64, D), 0) < lens[m, q]
+            gr[rows, :] = jnp.where(live, gr[rows, :].astype(F32), 0.0).astype(BF16)
     near = unit(1)
-    raw_landed(near)
     stage_p1(wa, near, near)
+    raw_step(3)
     stage_q2(wz, own, UNITS)
     stage_p2(wa, near, near)
     stage_q2(wa, own, own)
@@ -388,8 +392,8 @@
     for i in range(2):
         up(1, i).start()
         down(1, i).start()
+    raw_step(4)
     third = unit(2)
-    raw_landed(third)
     stage_p1(wa, third, third)
 
     @pl.loop(1, UNITS + 3)
@@ -400,12 +404,9 @@
                 u = unit(i + ahead)
                 stage(wa, u, u)
 
-        def first_stage(w, u, b):
-            raw_landed(u)
-            stage_p1(w, u, b)
-
         when_unit(0, stage_q1)
-        when_unit(2, first_stage)
+        pl.when(i == 2)(lambda: raw_landed(4))
+        when_unit(2, stage_p1)
         when_unit(1, stage_p2)
         k = -1
         for section in range(4):
@@ -494,32 +495,32 @@
         far = y2 if cc == 0 else x2
         to_plus, to_minus = (dyp, dym) if cc == 0 else (dxp, dxm)
         return (
-            remote(grow(cc, v, far, 0, 2), r1.at[v, 0], r1s.at[v, 0], r1r.at[v, 0], to_plus),
-            remote(grow(cc, v, far, 2, 2), r1.at[v, 1], r1s.at[v, 1], r1r.at[v, 1], to_minus),
+            remote(grow(cc, v, far, 0, 2), r1.at[v, 0], gsend.at[0], r1r.at[v, 0], to_plus),
+            remote(grow(cc, v, far, 2, 2), r1.at[v, 1], gsend.at[0], r1r.at[v, 1], to_minus),
         )
 
     def r2_copies(cc, v):
         plus, minus = (yp, ym) if cc == 0 else (xp, xm)
         to_plus, to_minus = (dyp, dym) if cc == 0 else (dxp, dxm)
         return (
-            remote(grow(cc, v, plus), r2.at[v, 0], r2s.at[v, 0], r2r.at[v, 0], to_plus),
-            remote(grow(cc, v, minus), r2.at[v, 1], r2s.at[v, 1], r2r.at[v, 1], to_minus),
+            remote(grow(cc, v, plus), r2.at[v, 0], gsend.at[1], r2r.at[v], to_plus),
+            remote(grow(cc, v, minus), r2.at[v, 1], gsend.at[1], r2r.at[v], to_minus),
         )
 
     def t1_copies(cc, v):
         far = x2 if cc == 0 else y2
         to_plus, to_minus = (dxp, dxm) if cc == 0 else (dyp, dym)
         return (
-            remote(gchip(cc, v, far, TOP), t1.at[v, 0], t1s.at[v, 0], t1r.at[v, 0], to_plus),
-            remote(gchip(cc, v, far, BOTTOM), t1.at[v, 1], t1s.at[v, 1], t1r.at[v, 1], to_minus),
+            remote(gchip(cc, v, far, TOP), t1.at[v, 0], gsend.at[2], t1r.at[v, 0], to_plus),
+            remote(gchip(cc, v, far, BOTTOM), t1.at[v, 1], gsend.at[2], t1r.at[v, 1], to_minus),
         )
 
     def t2_copies(cc, v):
         plus, minus = (xp, xm) if cc == 0 else (yp, ym)
         to_plus, to_minus = (dxp, dxm) if cc == 0 else (dyp, dym)
         return (
-            remote(gchip(cc, v, plus), t2.at[v, 0], t2s.at[v, 0], t2r.at[v, 0], to_plus),
-            remote(gchip(cc, v, minus), t2.at[v, 1], t2s.at[v, 1], t2r.at[v, 1], to_minus),
+            remote(gchip(cc, v, plus), t2.at[v, 0], gsend.at[3], t2r.at[v], to_plus),
+            remote(gchip(cc, v, minus), t2.at[v, 1], gsend.at[3], t2r.at[v], to_minus),
         )
 
     def add_into(ref, *others):
@@ -550,15 +551,18 @@
 
     def rs_c(v):
         def body(cc):
-            me = y if cc == 0 else x
-            arrive, leave = r2_copies(cc, v), t1_copies(cc, v)
-            arrive[0].wait_recv()
-            arrive[1].wait_recv()
-            for i in range(4):
-                block = gchip(cc, v, i)
-                add_into(block, r2.at[v, 0, i], r2.at[v, 1, i])
+            leave = t1_copies(cc, v)
+            remote(r2.at[v], r2.at[v], gsend.at[1], r2r.at[v], sib).wait_recv()
+
+            def add(i):
+                add_into(gchip(cc, v, i), r2.at[v, 0, i], r2.at[v, 1, i])
+
+            me, plus, minus, far = (x, xp, xm, x2) if cc == 0 else (y, yp, ym, y2)
+            add(far)
             for copy in leave:
                 copy.start()
+            for i in (plus, minus, me):
+                add(i)
 
         by_core(body)
 
@@ -576,11 +580,7 @@
         by_core(body)
 
     def rs_e(v):
-        def body(cc):
-            for copy in t2_copies(cc, v):
-                copy.wait_recv()
-
-        by_core(body)
+        remote(t2.at[v], t2.at[v], gsend.at[3], t2r.at[v], sib).wait_recv()
         return (
             xs[4 * v + y, x].astype(F32) + t2[v, 0].astype(F32) + t2[v, 1].astype(F32)
         )
@@ -590,6 +590,24 @@
     rs_a(v0)
     weight_term(v1)
     rs_a(v1)
+
+    def sent(block, sem):
+        remote(block, block, sem, sem, sib).wait_send()
+
+    for copy in gives(1 - c, my_rows):
+        copy.wait_send()
+    for way in range(2):
+        sent(wa.at[pl.ds(0, 7), 0, 0, 0, TOP], rsend.at[way])
+    sent(wa.at[0, :, pl.ds(0, 3)], psend.at[0])
+    sent(wz.at[0, 0, 0, pl.ds(0, 3)], psend.at[1])
+    sent(wa.at[pl.ds(0, 3)], qsend.at[0])
+    sent(wz.at[0, 0, pl.ds(0, 3)], qsend.at[1])
+    sent(wa.at[pl.ds(0, 4)], dsend.at[0])
+    sent(wz.at[0, 0], dsend.at[1])
+    sent(wz.at[pl.ds(0, 7), 0, pl.ds(0, 2)], usend)
+    sent(wz.at[pl.ds(0, 7), 0, pl.ds(0, 2)], lsend)
+    sent(wz.at[pl.ds(0, 7), :, pl.ds(0, 2)], esend)
+
     rs_b(v0)
     rs_b(v1)
     rs_c(v0)
@@ -600,63 +618,26 @@
     def cross(core):
         rows = pl.ds(pl.multiple_of(core * 32, 32), 32)
         dest = device(x, y, 2 * s + 1 - zl, core)
-        return remote(xs.at[4 * v0 + y, x, rows], z1.at[c], zsend.at[core], zrecv.at[c], dest)
+        return remote(xs.at[4 * v0 + y, x, rows], z1.at[c], zsend, zrecv, dest)
 
     cross(0).start()
     cross(1).start()
     sf[...] = rs_e(v1)
     last = remote(sf.at[sib_rows], o1, osend, orecv, sib)
     last.start()
-    for core in range(2):
-        remote(z1.at[core], z1.at[core], zsend.at[core], zrecv.at[core], sib).wait_recv()
+    remote(z1, z1, zsend, zrecv, sib).wait_recv()
     out_ref[:, mine] = sf[my_rows, :] + z1[c].astype(F32)
     last.wait_recv()
     out_ref[:, other] = o1[...] + z1[1 - c].astype(F32)
 
-    for copy in gives(1 - c, my_rows):
-        copy.wait_send()
-    for d in range(1, 8):
-        raw(d).wait_send()
-
-    @pl.loop(0, UNITS)
-    def _(u):
-        def body(cc):
-            for copy in p_copies(wa, cc, u, u) + q_copies(wa, cc, u, u):
-                copy.wait_send()
-            for i in range(4):
-                d_copy(wa, cc, u, u, i).wait_send()
-
-        by_core(body)
-
-    def own_sent(cc):
-        for copy in p_copies(wz, cc, own, UNITS) + q_copies(wz, cc, own, UNITS):
-            copy.wait_send()
-        for i in range(4):
-            d_copy(wz, cc, own, UNITS, i).wait_send()
-
-    by_core(own_sent)
-    for i in range(2):
-        for r in range(1, 4):
-            up(r, i).wait_send()
-            down(r, i).wait_send()
-        for slot in range(7):
-            e_copy(slot, i).wait_send()
-    up(4, 0).wait_send()
-    down(4, 1).wait_send()
     last.wait_send()
-    cross(0).wait_send()
-    cross(1).wait_send()
+    sent(z1, zsend)
     give_g.wait_send()
     normed_copy().wait_send()
-
-    @pl.loop(0, 2)
-    def _(v):
-        def body(cc):
-            for copies in (r1_copies, r2_copies, t1_copies, t2_copies):
-                for copy in copies(cc, v):
-                    copy.wait_send()
-
-        by_core(body)
+    sent(r1, gsend.at[0])
+    sent(r2, gsend.at[1])
+    sent(t1, gsend.at[2])
+    sent(t2, gsend.at[3])
 
 
 def local(inputs, weights, cotangents, lengths):
@@ -669,8 +650,8 @@
         in_specs=[
             pl.BlockSpec(memory_space=pl.ANY),
             vmem,
-            vmem,
-            pl.BlockSpec(memory_space=pltpu.SMEM),
+            pl.BlockSpec(memory_space=pl.ANY),
+            pl.BlockSpec(memory_space=pl.ANY),
         ],
         out_specs=vmem,
         scratch_shapes=[
@@ -691,35 +672,33 @@
             pltpu.VMEM((2, 32, HALF), BF16),
             pltpu.VMEM((64, HALF), F32),
             pltpu.VMEM((32, HALF), F32),
+            pltpu.SMEM((2, 2), jnp.int32),
+            dma((6,)),
+            dma((2,)),
+            dma((2,)),
+            dma((2,)),
+            dma((2, 4)),
+            dma,
+            dma((4, 2)),
+            dma,
+            dma((4, 2)),
+            dma,
+            dma((7,)),
+            dma((2,)),
+            dma((9, 3)),
+            dma((2,)),
+            dma((9, 4)),
+            dma((2,)),
+            dma((9,)),
+            dma((2,)),
+            dma((2,)),
             dma((4,)),
-            dma((2,)),
-            dma((2,)),
-            dma((7,)),
-            dma((8,)),
-            dma((4, 2)),
-            dma((4, 2)),
-            dma((4, 2)),
-            dma((4, 2)),
-            dma((7, 2)),
-            dma((7, 2)),
-            dma((9, 4)),
-            dma((9, 4)),
-            dma((9, 6)),
-            dma((9, 6)),
-            dma((9, 4)),
-            dma((9, 4)),
-            dma((2,)),
-            dma((2,)),
             dma((2, 2)),
+            dma((2,)),
             dma((2, 2)),
-            dma((2, 2)),
-            dma((2, 2)),
-            dma((2, 2)),
-            dma((2, 2)),
-            dma((2, 2)),
-            dma((2, 2)),
-            dma((2,)),
-            dma((2,)),
+            dma((2,)),
+            dma,
+            dma,
             dma,
             dma,
         ],

time: 150 us -> 150 us (level)
  no operation moved by 1% of the time
where the time goes in v7:
time: 150 us
  Pallas kernels  148 us (99%)
  local copies, waits for them, and re-layouts  1.67 us (1%)
    pallas_call x1, Pallas kernels, local(): pl.pallas_call(kernel, out_shape=jax.ShapeDtypeStruct((32, D), F32), in_s...  148 us

profile of v7, /device:TPU:1, one launch (start us, length us, event | category | flops | bytes accessed | tf_op | source)
XLA Modules:
  0.0 150.1 jit_solution(11717214762768431219)
XLA Ops:
  0.0 148.4 %shard_map.46 = f32[32,2048]{1,0:T(8,128)} custom-call(bf16[4,64,2048]{2,1,0:T(8,128)(2,1)} %bitcast.5, bf16[32,2048]{1,0:T(8,128)(2,1)} %bitcast.7, bf16[256,2048]{1,0:T(8,128)(2,1)} %bitcast.6, s32[2,2]{1,0:T(2,128)} %len_ref.1), custom_call_target="tpu_custom_call" | custom-call | flops 19327352832 | bytes 37748736 | tf_op jit(solution)/shard_map/pallas_call | solution.py:647
  148.4 1.7 %copy.6 = f32[1,32,2048]{2,1,0:T(8,128)} copy(f32[1,32,2048]{2,1,0:T(8,128)} %bitcast.4) | data formatting | bytes 524288

commit v8 on v7

--- a/solution.py
+++ b/solution.py
@@ -46,7 +46,7 @@
 
 def kernel(
     x_ref, w_ref, cot_ref, len_ref, out_ref,
-    wa, wz, xs, gd, iv, gp, nw, gw, gr, gn, r1, r2, t1, t2, z1, sf, o1,
+    wa, wz, xs, gd, ub, iv, gp, nw, gw, gr, ms, r1, r2, t1, t2, z1, sf, o1,
     lens, loc, xsend, xrecv, rsend, rrecv, usend, urecv, lsend, lrecv, esend, erecv,
     psend, precv, qsend, qrecv, dsend, drecv,
     nsend, nrecv, gsend, r1r, r2r, t1r, t2r, zsend, zrecv, osend, orecv,
@@ -313,6 +313,12 @@
         halves = [xs[2 * k + h, i // 2, at, :].astype(F32) for h in range(2)]
         return jnp.concatenate(halves, axis=1)
 
+    def lane_sums(v):
+        total = v[:, :128]
+        for i in range(1, HALF // 128):
+            total = total + v[:, i * 128 : (i + 1) * 128]
+        return total
+
     def forward(k):
         @pl.loop(0, 2)
         def _(uz):
@@ -338,11 +344,11 @@
             xf = section_rows(k, i)
             inv = lax.rsqrt(jnp.mean(xf * xf, axis=-1, keepdims=True) + EPS)
             iv[k, rows, :] = jnp.broadcast_to(inv, (32, 128))
-            gp[rows, :] = (xf * inv).astype(BF16)
+            gp[0, rows, :] = (xf * inv).astype(BF16)
 
         @pl.when(k == s)
         def _():
-            nw[c] = gp[...]
+            nw[c] = gp[0]
             normed_copy().start()
 
         @pl.loop(0, 2)
@@ -351,20 +357,27 @@
             w = jnp.concatenate(
                 [wa[2 * k + h].reshape(D, XY), wz[2 * k + h].reshape(D, Z)], axis=1
             )
-            u = jnp.dot(gp[...], w, preferred_element_type=F32)
+            u = jnp.dot(gp[0], w, preferred_element_type=F32)
             uu = u * u
             t = jnp.tanh((GELU_C * u) * (1.0 + GELU_A * uu))
             cdf = 0.5 * (1.0 + t)
-            gd[k, :, cols] = cdf + (0.5 * GELU_C) * u * (1.0 - t * t) * (
-                1.0 + (3.0 * GELU_A) * uu
-            )
+            slope = cdf + (0.5 * GELU_C) * u * (1.0 - t * t) * (1.0 + (3.0 * GELU_A) * uu)
 
             @pl.when(k < 3)
             def _():
-                nxt = jnp.minimum(k + 1, 3)
+                at = jnp.minimum(k, 2)
+                gd[at, :, cols] = slope
+                ub[at, :, cols] = u.astype(BF16)
                 before = xs[2 * k + h].reshape(ROWS, HALF)
                 after = (before.astype(F32) + u * cdf).astype(BF16)
-                xs[2 * nxt + h] = after.reshape(4, 64, HALF)
+                xs[2 * at + 2 + h] = after.reshape(4, 64, HALF)
+
+            @pl.when(k == 3)
+            def _():
+                pre = (gr[:, cols].astype(F32) * slope).astype(BF16)
+                gp[1, :, cols] = pre
+                term = lane_sums(pre.astype(F32) * u)
+                ms[...] = jnp.where(h == 0, term, ms[...] + term)
 
     own = unit(0)
     stage_p1(wz, own, UNITS)
@@ -427,17 +440,14 @@
 
         pl.when(i == 6)(relay_end)
 
-    @pl.loop(0, ROWS // 32)
-    def _(i):
-        rows = pl.ds(pl.multiple_of(i * 32, 32), 32)
-        gp[rows, :] = (gr[rows, :].astype(F32) * gd[3, rows, :]).astype(BF16)
-
     @pl.loop(0, 3 - s)
     def _(step):
         k = 3 - step
-
-        @pl.loop(0, 2)
-        def _(j):
+        now = lax.rem(step + 1, 2)
+        inv = iv[k][:, :1]
+        factor = inv * inv * (jnp.sum(ms[...], axis=-1, keepdims=True) * (1.0 / D))
+        sums = None
+        for j in range(2):
             tile = jnp.concatenate(
                 [
                     w[2 * k + h, j].reshape(HALF, width)
@@ -446,24 +456,22 @@
                 ],
                 axis=1,
             )
-            gn[:, part(j, 0, HALF)] = lax.dot_general(
-                gp[...], tile, (((1,), (1,)), ((), ())), preferred_element_type=F32
+            g = lax.dot_general(
+                gp[now], tile, (((1,), (1,)), ((), ())), preferred_element_type=F32
             )
-
-        @pl.loop(0, ROWS // 32)
-        def _(i):
-            rows = pl.ds(pl.multiple_of(i * 32, 32), 32)
-            xf = section_rows(k, i)
-            g = gn[rows, :]
-            inv = iv[k, rows, :][:, :1]
-            mean = jnp.mean(g * xf, axis=-1, keepdims=True)
-            grad = gr[rows, :].astype(F32) + inv * g - xf * (inv * inv * inv * mean)
-            grad = grad.astype(BF16)
-            gr[rows, :] = grad
-            gp[rows, :] = (grad.astype(F32) * gd[k - 1, rows, :]).astype(BF16)
-
-    gw[c] = gp[:, mine]
-    give_g = remote(gp.at[:, other], gw.at[c], nsend.at[1], nrecv.at[1], sib)
+            cols = pl.ds(j * HALF, HALF)
+            xf = xs[2 * k + j].reshape(ROWS, HALF).astype(F32)
+            grad = (gr[:, cols].astype(F32) + inv * g - xf * factor).astype(BF16)
+            gr[:, cols] = grad
+            pre = (grad.astype(F32) * gd[k - 1, :, cols]).astype(BF16)
+            gp[1 - now, :, cols] = pre
+            term = lane_sums(pre.astype(F32) * ub[k - 1, :, cols].astype(F32))
+            sums = term if sums is None else sums + term
+        ms[...] = sums
+
+    last_gp = lax.rem(s, 2)
+    gw[c] = gp[last_gp, :, mine]
+    give_g = remote(gp.at[last_gp, :, other], gw.at[c], nsend.at[1], nrecv.at[1], sib)
     give_g.start()
 
     remote(nw.at[1 - c], nw.at[1 - c], nsend.at[0], nrecv.at[0], sib).wait_recv()
@@ -658,13 +666,14 @@
             pltpu.VMEM((8, 2, 4, 4, 64, XY), BF16),
             pltpu.VMEM((8, 2, 4, 4, 64, Z), BF16),
             pltpu.VMEM((8, 4, 64, HALF), BF16),
-            pltpu.VMEM((4, ROWS, D), F32),
+            pltpu.VMEM((3, ROWS, D), F32),
+            pltpu.VMEM((3, ROWS, D), BF16),
             pltpu.VMEM((4, ROWS, 128), F32),
-            pltpu.VMEM((ROWS, D), BF16),
+            pltpu.VMEM((2, ROWS, D), BF16),
             pltpu.VMEM((2, ROWS, D), BF16),
             pltpu.VMEM((2, ROWS, HALF), BF16),
             pltpu.VMEM((ROWS, D), BF16),
-            pltpu.VMEM((ROWS, D), F32),
+            pltpu.VMEM((ROWS, 128), F32),
             pltpu.VMEM((2, 2, 2, 64, HALF), BF16),
             pltpu.VMEM((2, 2, 4, 64, HALF), BF16),
             pltpu.VMEM((2, 2, 32, HALF), BF16),

time: 150 us -> 146 us (0.973)
  Pallas kernels: 148 us -> 144 us
    pallas_call x1, Pallas kernels: 148 us -> 144 us  [local(): pl.pallas_call(kernel, out_shape=jax.ShapeDtypeStruct((32, D), F32), in_s...]
where the time goes in v8:
time: 146 us
  Pallas kernels  144 us (99%)
  local copies, waits for them, and re-layouts  1.67 us (1%)
    pallas_call x1, Pallas kernels, local(): pl.pallas_call(kernel, out_shape=jax.ShapeDtypeStruct((32, D), F32), in_s...  144 us

profile of v8, /device:TPU:1, one launch (start us, length us, event | category | flops | bytes accessed | tf_op | source)
XLA Modules:
  0.0 146.0 jit_solution(4250063360757922128)
XLA Ops:
  0.0 144.3 %shard_map.46 = f32[32,2048]{1,0:T(8,128)} custom-call(bf16[4,64,2048]{2,1,0:T(8,128)(2,1)} %bitcast.5, bf16[32,2048]{1,0:T(8,128)(2,1)} %bitcast.7, bf16[256,2048]{1,0:T(8,128)(2,1)} %bitcast.6, s32[2,2]{1,0:T(2,128)} %len_ref.1), custom_call_target="tpu_custom_call" | custom-call | flops 19327352832 | bytes 37748736 | tf_op jit(solution)/shard_map/pallas_call | solution.py:655
  144.3 1.7 %copy.6 = f32[1,32,2048]{2,1,0:T(8,128)} copy(f32[1,32,2048]{2,1,0:T(8,128)} %bitcast.4) | data formatting | bytes 524288

commit v9 on v8

--- a/solution.py
+++ b/solution.py
@@ -17,6 +17,8 @@
 D = 2048
 ROWS = 256
 HALF = 1024
+QUART = 512
+CS = (pl.ds(0, QUART), pl.ds(QUART, QUART))
 XY = 768
 Z = HALF - XY
 UNITS = 8
@@ -46,10 +48,10 @@
 
 def kernel(
     x_ref, w_ref, cot_ref, len_ref, out_ref,
-    wa, wz, xs, gd, ub, iv, gp, nw, gw, gr, ms, r1, r2, t1, t2, z1, sf, o1,
+    wa, wz, xs, gd, ub, iv, gp, nw, gw, gr, ms, r1, r2, t1, t2, u2, z1, o1,
     lens, loc, xsend, xrecv, rsend, rrecv, usend, urecv, lsend, lrecv, esend, erecv,
     psend, precv, qsend, qrecv, dsend, drecv,
-    nsend, nrecv, gsend, r1r, r2r, t1r, t2r, zsend, zrecv, osend, orecv,
+    nsend, nrecv, gsend, r1r, r2r, t1r, t2r, u2r, zsend, zrecv, osend, orecv,
 ):
     s, zl, x, y, c = position()
     z = 2 * s + zl
@@ -63,7 +65,13 @@
     barrier = pltpu.get_barrier_semaphore()
     above, below = device(x, y, lax.rem(z + 1, 8), c), device(x, y, lax.rem(z + 7, 8), c)
     pair_other = device(x, y, 2 * s + 1 - zl, 1 - c)
-    for partner in (dxp, dxm, dyp, dym, above, below, sib, pair_other):
+    def crossed(plus):
+        return device(
+            jnp.where(c == 0, x, xp if plus else xm), jnp.where(c == 0, yp if plus else ym, y), z, 1 - c
+        )
+
+    cross_plus, cross_minus = crossed(True), crossed(False)
+    for partner in (dxp, dxm, dyp, dym, above, below, sib, pair_other, cross_plus, cross_minus):
         pl.semaphore_signal(barrier, inc=1, device_id=partner, device_id_type=MESH)
 
     def part(core, first, width):
@@ -92,7 +100,7 @@
     ]
     for copy in in_w:
         copy.start()
-    pl.semaphore_wait(barrier, 8)
+    pl.semaphore_wait(barrier, 10)
 
     def gives(core, rows):
         kh = 2 * s + core
@@ -470,66 +478,90 @@
         ms[...] = sums
 
     last_gp = lax.rem(s, 2)
-    gw[c] = gp[last_gp, :, mine]
-    give_g = remote(gp.at[last_gp, :, other], gw.at[c], nsend.at[1], nrecv.at[1], sib)
-    give_g.start()
-
+    def column_part(core, hc):
+        return part(core, hc * QUART, QUART)
+
+    def give_g(hc):
+        return remote(
+            gp.at[last_gp, :, column_part(1 - c, hc)], gw.at[c, :, CS[hc]],
+            nsend.at[1 + hc], nrecv.at[1 + hc], sib,
+        )
+
+    for hc in range(2):
+        give_g(hc).start()
+    for hc in range(2):
+        gw[c, :, CS[hc]] = gp[last_gp, :, column_part(c, hc)]
     remote(nw.at[1 - c], nw.at[1 - c], nsend.at[0], nrecv.at[0], sib).wait_recv()
-    remote(gw.at[1 - c], gw.at[1 - c], nsend.at[1], nrecv.at[1], sib).wait_recv()
-
-    def weight_term(v):
-        @pl.loop(0, 4)
+
+    v0, v1 = 1 - zl, zl
+    v_of = (v0, v0, v1, v1)
+
+    def weight_term(q):
+        v, cs = v_of[q], CS[q % 2]
+
+        @pl.loop(0, 2)
         def _(j):
-            cols = pl.ds(pl.multiple_of(v * HALF + j * 256, 256), 256)
-            total = None
-            for half in range(2):
-                part = lax.dot_general(
-                    nw[half, :, cols], gw[half], (((0,), (0,)), ((), ())),
-                    preferred_element_type=F32,
-                )
-                total = part if total is None else total + part
-            xs[4 * v + j] = total.astype(BF16).reshape(4, 64, HALF)
-
-    def grow(cc, v, i, first=0, count=4):
+            rows = pl.ds(pl.multiple_of(v * HALF + j * 512, 512), 512)
+            left = nw[:, :, rows].reshape(2 * ROWS, 512)
+            right = gw[:, :, cs].reshape(2 * ROWS, QUART)
+            total = lax.dot_general(
+                left, right, (((0,), (0,)), ((), ())), preferred_element_type=F32
+            )
+            xs[pl.ds(4 * v + 2 * j, 2), :, :, cs] = total.astype(BF16).reshape(2, 4, 64, QUART)
+
+    def grow(cc, q, i, first=0, count=4):
+        v, cs = v_of[q], CS[q % 2]
         if cc == 0:
-            return xs.at[4 * v + i, pl.ds(first, count)]
-        return xs.at[pl.ds(4 * v + first, count), i]
-
-    def gchip(cc, v, i, part=None):
-        at = (4 * v + y, i) if cc == 0 else (4 * v + i, x)
-        return xs.at[at] if part is None else xs.at[at + (part,)]
-
-    def r1_copies(cc, v):
-        far = y2 if cc == 0 else x2
-        to_plus, to_minus = (dyp, dym) if cc == 0 else (dxp, dxm)
+            return xs.at[4 * v + i, pl.ds(first, count), :, cs]
+        return xs.at[pl.ds(4 * v + first, count), i, :, cs]
+
+    def gchip(cc, q, i, rows=None):
+        v, cs = v_of[q], CS[q % 2]
+        rows = pl.ds(0, 64) if rows is None else rows
+        return xs.at[4 * v + y, i, rows, cs] if cc == 0 else xs.at[4 * v + i, x, rows, cs]
+
+    def q_axis(cc):
+        return (y, yp, ym, y2, dyp, dym) if cc == 0 else (x, xp, xm, x2, dxp, dxm)
+
+    def p_axis(cc):
+        return (x, xp, xm, x2, dxp, dxm) if cc == 0 else (y, yp, ym, y2, dyp, dym)
+
+    def r1_copies(cc, q):
+        _, _, _, far, to_plus, to_minus = q_axis(cc)
         return (
-            remote(grow(cc, v, far, 0, 2), r1.at[v, 0], gsend.at[0], r1r.at[v, 0], to_plus),
-            remote(grow(cc, v, far, 2, 2), r1.at[v, 1], gsend.at[0], r1r.at[v, 1], to_minus),
-        )
-
-    def r2_copies(cc, v):
-        plus, minus = (yp, ym) if cc == 0 else (xp, xm)
-        to_plus, to_minus = (dyp, dym) if cc == 0 else (dxp, dxm)
+            remote(grow(cc, q, far, 0, 2), r1.at[q, 0], gsend.at[0], r1r.at[q, 0], to_plus),
+            remote(grow(cc, q, far, 2, 2), r1.at[q, 1], gsend.at[0], r1r.at[q, 1], to_minus),
+        )
+
+    def r2_copies(cc, q):
+        _, plus, minus, _, to_plus, to_minus = q_axis(cc)
         return (
-            remote(grow(cc, v, plus), r2.at[v, 0], gsend.at[1], r2r.at[v], to_plus),
-            remote(grow(cc, v, minus), r2.at[v, 1], gsend.at[1], r2r.at[v], to_minus),
-        )
-
-    def t1_copies(cc, v):
-        far = x2 if cc == 0 else y2
-        to_plus, to_minus = (dxp, dxm) if cc == 0 else (dyp, dym)
+            remote(grow(cc, q, plus), r2.at[q, 0], gsend.at[1], r2r.at[q], to_plus),
+            remote(grow(cc, q, minus), r2.at[q, 1], gsend.at[1], r2r.at[q], to_minus),
+        )
+
+    def t1_copies(cc, q):
+        _, _, _, far, to_plus, to_minus = p_axis(cc)
         return (
-            remote(gchip(cc, v, far, TOP), t1.at[v, 0], gsend.at[2], t1r.at[v, 0], to_plus),
-            remote(gchip(cc, v, far, BOTTOM), t1.at[v, 1], gsend.at[2], t1r.at[v, 1], to_minus),
-        )
-
-    def t2_copies(cc, v):
-        plus, minus = (xp, xm) if cc == 0 else (yp, ym)
-        to_plus, to_minus = (dxp, dxm) if cc == 0 else (dyp, dym)
-        return (
-            remote(gchip(cc, v, plus), t2.at[v, 0], gsend.at[3], t2r.at[v], to_plus),
-            remote(gchip(cc, v, minus), t2.at[v, 1], gsend.at[3], t2r.at[v], to_minus),
-        )
+            remote(gchip(cc, q, far, TOP), t1.at[q, 0], gsend.at[2], t1r.at[q, 0], to_plus),
+            remote(gchip(cc, q, far, BOTTOM), t1.at[q, 1], gsend.at[2], t1r.at[q, 1], to_minus),
+        )
+
+    def t2_copies(cc, q, way):
+        _, plus, minus, _, to_plus, to_minus = p_axis(cc)
+        block, dest = ((plus, to_plus), (minus, to_minus))[way]
+        if q < 2:
+            return [
+                remote(gchip(cc, q, block), t2.at[q, way], gsend.at[3], t2r.at[q], dest)
+            ]
+        at = (block, y) if cc == 0 else (x, block)
+        return [
+            remote(
+                gchip(cc, q, block, (TOP, BOTTOM)[core]), u2.at[q - 2, cc, way],
+                gsend.at[4], u2r.at[q - 2], device(*at, z, core),
+            )
+            for core in range(2)
+        ]
 
     def add_into(ref, *others):
         total = ref[...].astype(F32)
@@ -537,67 +569,92 @@
             total = total + more[...].astype(F32)
         ref[...] = total.astype(BF16)
 
-    def rs_a(v):
-        def body(cc):
-            for copy in r1_copies(cc, v):
+    def rs_a(q):
+        def body(cc):
+            for copy in r1_copies(cc, q):
                 copy.start()
 
         by_core(body)
 
-    def rs_b(v):
-        def body(cc):
-            plus, minus = (yp, ym) if cc == 0 else (xp, xm)
-            arrive, leave = r1_copies(cc, v), r2_copies(cc, v)
+    def rs_b(q):
+        def body(cc):
+            _, plus, minus, _, _, _ = q_axis(cc)
+            arrive, leave = r1_copies(cc, q), r2_copies(cc, q)
             arrive[0].wait_recv()
-            add_into(grow(cc, v, plus, 0, 2), r1.at[v, 0])
+            add_into(grow(cc, q, plus, 0, 2), r1.at[q, 0])
             leave[0].start()
             arrive[1].wait_recv()
-            add_into(grow(cc, v, minus, 2, 2), r1.at[v, 1])
+            add_into(grow(cc, q, minus, 2, 2), r1.at[q, 1])
             leave[1].start()
 
         by_core(body)
 
-    def rs_c(v):
-        def body(cc):
-            leave = t1_copies(cc, v)
-            remote(r2.at[v], r2.at[v], gsend.at[1], r2r.at[v], sib).wait_recv()
+    def own_part(q):
+        block = xs.at[4 * v_of[q] + y, x, sib_rows, CS[q % 2]]
+        return remote(block, o1.at[q - 2], osend, orecv.at[q - 2], sib)
+
+    def rs_c(q):
+        def body(cc):
+            me, plus, minus, far, _, _ = p_axis(cc)
+            remote(r2.at[q], r2.at[q], gsend.at[1], r2r.at[q], sib).wait_recv()
 
             def add(i):
-                add_into(gchip(cc, v, i), r2.at[v, 0, i], r2.at[v, 1, i])
-
-            me, plus, minus, far = (x, xp, xm, x2) if cc == 0 else (y, yp, ym, y2)
+                add_into(gchip(cc, q, i), r2.at[q, 0, i], r2.at[q, 1, i])
+
             add(far)
-            for copy in leave:
+            for copy in t1_copies(cc, q):
                 copy.start()
-            for i in (plus, minus, me):
-                add(i)
-
-        by_core(body)
-
-    def rs_d(v):
-        def body(cc):
-            plus, minus = (xp, xm) if cc == 0 else (yp, ym)
-            arrive, leave = t1_copies(cc, v), t2_copies(cc, v)
+            add(plus)
+            add(minus)
+            add(me)
+            if q >= 2:
+                own_part(q).start()
+
+        by_core(body)
+
+    def rs_d(q):
+        def body(cc):
+            _, plus, minus, _, _, _ = p_axis(cc)
+            arrive = t1_copies(cc, q)
             arrive[0].wait_recv()
-            add_into(gchip(cc, v, plus, TOP), t1.at[v, 0])
-            leave[0].start()
+            add_into(gchip(cc, q, plus, TOP), t1.at[q, 0])
+            for copy in t2_copies(cc, q, 0):
+                copy.start()
             arrive[1].wait_recv()
-            add_into(gchip(cc, v, minus, BOTTOM), t1.at[v, 1])
-            leave[1].start()
-
-        by_core(body)
-
-    def rs_e(v):
-        remote(t2.at[v], t2.at[v], gsend.at[3], t2r.at[v], sib).wait_recv()
-        return (
-            xs[4 * v + y, x].astype(F32) + t2[v, 0].astype(F32) + t2[v, 1].astype(F32)
-        )
-
-    v0, v1 = 1 - zl, zl
-    weight_term(v0)
-    rs_a(v0)
-    weight_term(v1)
-    rs_a(v1)
+            add_into(gchip(cc, q, minus, BOTTOM), t1.at[q, 1])
+            for copy in t2_copies(cc, q, 1):
+                copy.start()
+
+        by_core(body)
+
+    def cross(q, core):
+        rows = (TOP, BOTTOM)[core]
+        block = xs.at[4 * v0 + y, x, rows, CS[q]]
+        dest = device(x, y, 2 * s + 1 - zl, core)
+        return remote(block, z1.at[c, :, CS[q]], zsend, zrecv, dest)
+
+    def rs_e(q):
+        remote(t2.at[q], t2.at[q], gsend.at[3], t2r.at[q], sib).wait_recv()
+        add_into(xs.at[4 * v0 + y, x, :, CS[q]], t2.at[q, 0], t2.at[q, 1])
+        cross(q, 0).start()
+        cross(q, 1).start()
+
+    def finish(q):
+        hc = q - 2
+        remote(o1.at[hc], o1.at[hc], osend, orecv.at[hc], sib).wait_recv()
+        remote(u2.at[hc], u2.at[hc], gsend.at[4], u2r.at[hc], sib).wait_recv()
+        for core, own_ in ((c, xs[4 * v1 + y, x, my_rows, CS[hc]]), (1 - c, o1[hc])):
+            total = own_.astype(F32) + z1[core, :, CS[hc]].astype(F32)
+            for way in range(2):
+                total = total + u2[hc, core, way].astype(F32)
+            out_ref[:, column_part(core, hc)] = total
+
+    for q in range(4):
+        if q < 2:
+            got = gw.at[1 - c, :, CS[q]]
+            remote(got, got, nsend.at[1 + q], nrecv.at[1 + q], sib).wait_recv()
+        weight_term(q)
+        rs_a(q)
 
     def sent(block, sem):
         remote(block, block, sem, sem, sib).wait_send()
@@ -616,36 +673,32 @@
     sent(wz.at[pl.ds(0, 7), 0, pl.ds(0, 2)], lsend)
     sent(wz.at[pl.ds(0, 7), :, pl.ds(0, 2)], esend)
 
-    rs_b(v0)
-    rs_b(v1)
-    rs_c(v0)
-    rs_c(v1)
-    rs_d(v0)
-    rs_d(v1)
-    xs[4 * v0 + y, x] = rs_e(v0).astype(BF16)
-    def cross(core):
-        rows = pl.ds(pl.multiple_of(core * 32, 32), 32)
-        dest = device(x, y, 2 * s + 1 - zl, core)
-        return remote(xs.at[4 * v0 + y, x, rows], z1.at[c], zsend, zrecv, dest)
-
-    cross(0).start()
-    cross(1).start()
-    sf[...] = rs_e(v1)
-    last = remote(sf.at[sib_rows], o1, osend, orecv, sib)
-    last.start()
+    for q in range(4):
+        rs_b(q)
+    rs_c(0)
+    rs_c(1)
+    rs_d(0)
+    rs_c(2)
+    rs_d(1)
+    rs_e(0)
+    rs_c(3)
+    rs_d(2)
+    rs_e(1)
+    rs_d(3)
     remote(z1, z1, zsend, zrecv, sib).wait_recv()
-    out_ref[:, mine] = sf[my_rows, :] + z1[c].astype(F32)
-    last.wait_recv()
-    out_ref[:, other] = o1[...] + z1[1 - c].astype(F32)
-
-    last.wait_send()
+    finish(2)
+    finish(3)
+
+    sent(o1, osend)
     sent(z1, zsend)
-    give_g.wait_send()
+    give_g(0).wait_send()
+    give_g(1).wait_send()
     normed_copy().wait_send()
     sent(r1, gsend.at[0])
     sent(r2, gsend.at[1])
     sent(t1, gsend.at[2])
     sent(t2, gsend.at[3])
+    sent(u2, gsend.at[4])
 
 
 def local(inputs, weights, cotangents, lengths):
@@ -674,13 +727,13 @@
             pltpu.VMEM((2, ROWS, HALF), BF16),
             pltpu.VMEM((ROWS, D), BF16),
             pltpu.VMEM((ROWS, 128), F32),
-            pltpu.VMEM((2, 2, 2, 64, HALF), BF16),
-            pltpu.VMEM((2, 2, 4, 64, HALF), BF16),
-            pltpu.VMEM((2, 2, 32, HALF), BF16),
-            pltpu.VMEM((2, 2, 64, HALF), BF16),
+            pltpu.VMEM((4, 2, 2, 64, QUART), BF16),
+            pltpu.VMEM((4, 2, 4, 64, QUART), BF16),
+            pltpu.VMEM((4, 2, 32, QUART), BF16),
+            pltpu.VMEM((2, 2, 64, QUART), BF16),
+            pltpu.VMEM((2, 2, 2, 32, QUART), BF16),
             pltpu.VMEM((2, 32, HALF), BF16),
-            pltpu.VMEM((64, HALF), F32),
-            pltpu.VMEM((32, HALF), F32),
+            pltpu.VMEM((2, 32, QUART), BF16),
             pltpu.SMEM((2, 2), jnp.int32),
             dma((6,)),
             dma((2,)),
@@ -699,17 +752,18 @@
             dma((9, 4)),
             dma((2,)),
             dma((9,)),
-            dma((2,)),
-            dma((2,)),
+            dma((3,)),
+            dma((3,)),
+            dma((5,)),
+            dma((4, 2)),
             dma((4,)),
-            dma((2, 2)),
-            dma((2,)),
-            dma((2, 2)),
+            dma((4, 2)),
+            dma((2,)),
             dma((2,)),
             dma,
             dma,
             dma,
-            dma,
+            dma((2,)),
         ],
         compiler_params=pltpu.CompilerParams(
             collective_id=0, has_side_effects=True, vmem_limit_bytes=63 * 2**20

time: 146 us -> 145 us (level)
    pallas_call x1, Pallas kernels: 144 us -> 143 us  [local(): pl.pallas_call(kernel, out_shape=jax.ShapeDtypeStruct((32, D), F32), in_s...]
where the time goes in v9:
time: 145 us; the launch traced here: 144 us
  Pallas kernels  143 us (99%)
  local copies, waits for them, and re-layouts  1.67 us (1%)
    pallas_call x1, Pallas kernels, local(): pl.pallas_call(kernel, out_shape=jax.ShapeDtypeStruct((32, D), F32), in_s...  143 us

profile of v9, /device:TPU:1, one launch (start us, length us, event | category | flops | bytes accessed | tf_op | source)
XLA Modules:
  0.0 144.5 jit_solution(6167794813927821370)
XLA Ops:
  0.0 142.8 %shard_map.46 = f32[32,2048]{1,0:T(8,128)} custom-call(bf16[4,64,2048]{2,1,0:T(8,128)(2,1)} %bitcast.5, bf16[32,2048]{1,0:T(8,128)(2,1)} %bitcast.7, bf16[256,2048]{1,0:T(8,128)(2,1)} %bitcast.6, s32[2,2]{1,0:T(2,128)} %len_ref.1), custom_call_target="tpu_custom_call" | custom-call | flops 19327352832 | bytes 37748736 | tf_op jit(solution)/shard_map/pallas_call | solution.py:708
  142.8 1.7 %copy.6 = f32[1,32,2048]{2,1,0:T(8,128)} copy(f32[1,32,2048]{2,1,0:T(8,128)} %bitcast.4) | data formatting | bytes 524288

commit v10 on v9

--- a/solution.py
+++ b/solution.py
@@ -22,7 +22,7 @@
 XY = 768
 Z = HALF - XY
 UNITS = 8
-READY = ((3, 6, 7, 9), (6, 7, 8, 9), (7, 8, 9, 10), (6, 7, 9, 10))
+READY = ((4, 6, 8), (6, 7, 8), (8, 9), (6, 8))
 FIRST, SECOND = pl.ds(0, 2), pl.ds(2, 2)
 TOP, BOTTOM = pl.ds(0, 32), pl.ds(32, 32)
 
@@ -408,7 +408,6 @@
     raw_step(3)
     stage_q2(wz, own, UNITS)
     stage_p2(wa, near, near)
-    stage_q2(wa, own, own)
     stage_f(wz, own, UNITS)
     for i in range(2):
         up(1, i).start()
@@ -417,7 +416,7 @@
     third = unit(2)
     stage_p1(wa, third, third)
 
-    @pl.loop(1, UNITS + 3)
+    @pl.loop(1, UNITS + 2)
     def _(i):
         def when_unit(ahead, stage):
             @pl.when((i + ahead >= 0) & (i + ahead < UNITS))
@@ -429,24 +428,32 @@
         pl.when(i == 2)(lambda: raw_landed(4))
         when_unit(2, stage_p1)
         when_unit(1, stage_p2)
+        when_unit(-1, stage_q2)
         k = -1
         for section in range(4):
-            for number in range(4):
-                k = jnp.where((s == section) & (i == READY[section][number]), number, k)
+            for number, step in enumerate(READY[section]):
+                k = jnp.where((s == section) & (i == step), number, k)
         pl.when(k >= 0)(lambda: forward(jnp.maximum(k, 0)))
-        when_unit(0, stage_q2)
-        when_unit(-1, stage_f)
-        pl.when(i == 1)(lambda: relay(1, 0))
-        pl.when(i == 2)(lambda: relay(1, 1))
-        pl.when(i == 3)(lambda: relay(2, 0))
-        pl.when(i == 4)(lambda: relay(2, 1))
-
-        @pl.when(i == 5)
+        when_unit(-2, stage_f)
+        pl.when(i == 2)(lambda: relay(1, 0))
+
+        @pl.when(i == 3)
         def _():
+            relay(1, 1)
+            relay(2, 0)
+
+        @pl.when(i == 4)
+        def _():
+            relay(2, 1)
             relay(3, 0)
-            relay(3, 1)
-
+
+        pl.when(i == 5)(lambda: relay(3, 1))
         pl.when(i == 6)(relay_end)
+
+    done = jnp.int32(len(READY[0]))
+    for section in range(1, 4):
+        done = jnp.where(s == section, len(READY[section]), done)
+    pl.loop(done, 4)(forward)
 
     @pl.loop(0, 3 - s)
     def _(step):

time: 145 us -> 138 us (0.952)
  Pallas kernels: 143 us -> 136 us
    pallas_call x1, Pallas kernels: 143 us -> 136 us  [local(): pl.pallas_call(kernel, out_shape=jax.ShapeDtypeStruct((32, D), F32), in_s...]
where the time goes in v10:
time: 138 us
  Pallas kernels  136 us (99%)
  local copies, waits for them, and re-layouts  1.67 us (1%)
    pallas_call x1, Pallas kernels, local(): pl.pallas_call(kernel, out_shape=jax.ShapeDtypeStruct((32, D), F32), in_s...  136 us

profile of v10, /device:TPU:1, one launch (start us, length us, event | category | flops | bytes accessed | tf_op | source)
XLA Modules:
  0.0 137.8 jit_solution(5958454098590533208)
XLA Ops:
  0.0 136.1 %shard_map.46 = f32[32,2048]{1,0:T(8,128)} custom-call(bf16[4,64,2048]{2,1,0:T(8,128)(2,1)} %bitcast.5, bf16[32,2048]{1,0:T(8,128)(2,1)} %bitcast.7, bf16[256,2048]{1,0:T(8,128)(2,1)} %bitcast.6, s32[2,2]{1,0:T(2,128)} %len_ref.1), custom_call_target="tpu_custom_call" | custom-call | flops 19327352832 | bytes 37748736 | tf_op jit(solution)/shard_map/pallas_call | solution.py:715
  136.1 1.7 %copy.6 = f32[1,32,2048]{2,1,0:T(8,128)} copy(f32[1,32,2048]{2,1,0:T(8,128)} %bitcast.4) | data formatting | bytes 524288

commit v11 on v10

--- a/solution.py
+++ b/solution.py
@@ -327,25 +327,7 @@
             total = total + v[:, i * 128 : (i + 1) * 128]
         return total
 
-    def forward(k):
-        @pl.loop(0, 2)
-        def _(uz):
-            u = 2 * k + uz
-
-            block = wa.at[2 * k + 1 - c, uz]
-            remote(block, block, dsend.at[0], drecv.at[u], sib).wait_recv()
-            z_block = wz.at[2 * k + 1 - c, uz]
-
-            @pl.when(u == z)
-            def _():
-                remote(z_block, z_block, dsend.at[1], drecv.at[UNITS], sib).wait_recv()
-
-            @pl.when(u != z)
-            def _():
-                d = lax.rem(u - z + 8, 8)
-                slot = jnp.where(d < 4, 2 + d, jnp.where(d == 4, 6, 7 - d))
-                remote(z_block, z_block, esend, erecv.at[slot], sib).wait_recv()
-
+    def norm(k):
         @pl.loop(0, ROWS // 32)
         def _(i):
             rows = pl.ds(pl.multiple_of(i * 32, 32), 32)
@@ -359,33 +341,61 @@
             nw[c] = gp[0]
             normed_copy().start()
 
+    def arrived(k):
+        @pl.loop(0, 2)
+        def _(uz):
+            u = 2 * k + uz
+
+            block = wa.at[2 * k + 1 - c, uz]
+            remote(block, block, dsend.at[0], drecv.at[u], sib).wait_recv()
+            z_block = wz.at[2 * k + 1 - c, uz]
+
+            @pl.when(u == z)
+            def _():
+                remote(z_block, z_block, dsend.at[1], drecv.at[UNITS], sib).wait_recv()
+
+            @pl.when(u != z)
+            def _():
+                d = lax.rem(u - z + 8, 8)
+                slot = jnp.where(d < 4, 2 + d, jnp.where(d == 4, 6, 7 - d))
+                remote(z_block, z_block, esend, erecv.at[slot], sib).wait_recv()
+
+    def preact(k, h):
+        w = jnp.concatenate([wa[2 * k + h].reshape(D, XY), wz[2 * k + h].reshape(D, Z)], axis=1)
+        u = jnp.dot(gp[0], w, preferred_element_type=F32)
+        uu = u * u
+        t = jnp.tanh((GELU_C * u) * (1.0 + GELU_A * uu))
+        cdf = 0.5 * (1.0 + t)
+        slope = cdf + (0.5 * GELU_C) * u * (1.0 - t * t) * (1.0 + (3.0 * GELU_A) * uu)
+        return u, cdf, slope
+
+    def forward(k):
+        arrived(k)
+
         @pl.loop(0, 2)
         def _(h):
             cols = part(h, 0, HALF)
-            w = jnp.concatenate(
-                [wa[2 * k + h].reshape(D, XY), wz[2 * k + h].reshape(D, Z)], axis=1
-            )
-            u = jnp.dot(gp[0], w, preferred_element_type=F32)
-            uu = u * u
-            t = jnp.tanh((GELU_C * u) * (1.0 + GELU_A * uu))
-            cdf = 0.5 * (1.0 + t)
-            slope = cdf + (0.5 * GELU_C) * u * (1.0 - t * t) * (1.0 + (3.0 * GELU_A) * uu)
-
-            @pl.when(k < 3)
-            def _():
-                at = jnp.minimum(k, 2)
-                gd[at, :, cols] = slope
-                ub[at, :, cols] = u.astype(BF16)
-                before = xs[2 * k + h].reshape(ROWS, HALF)
-                after = (before.astype(F32) + u * cdf).astype(BF16)
-                xs[2 * at + 2 + h] = after.reshape(4, 64, HALF)
-
-            @pl.when(k == 3)
-            def _():
-                pre = (gr[:, cols].astype(F32) * slope).astype(BF16)
-                gp[1, :, cols] = pre
-                term = lane_sums(pre.astype(F32) * u)
-                ms[...] = jnp.where(h == 0, term, ms[...] + term)
+            u, cdf, slope = preact(k, h)
+            gd[k, :, cols] = slope
+            ub[k, :, cols] = u.astype(BF16)
+            before = xs[2 * k + h].reshape(ROWS, HALF)
+            after = (before.astype(F32) + u * cdf).astype(BF16)
+            xs[2 * k + 2 + h] = after.reshape(4, 64, HALF)
+
+        pl.when(k < 2)(lambda: norm(jnp.minimum(k + 1, 2)))
+
+    def forward_last():
+        norm(3)
+        arrived(3)
+        sums = None
+        for h in range(2):
+            cols = pl.ds(h * HALF, HALF)
+            u, _, slope = preact(3, h)
+            pre = (gr[:, cols].astype(F32) * slope).astype(BF16)
+            gp[1, :, cols] = pre
+            term = lane_sums(pre.astype(F32) * u)
+            sums = term if sums is None else sums + term
+        ms[...] = sums
 
     own = unit(0)
     stage_p1(wz, own, UNITS)
@@ -415,6 +425,7 @@
     raw_step(4)
     third = unit(2)
     stage_p1(wa, third, third)
+    norm(0)
 
     @pl.loop(1, UNITS + 2)
     def _(i):
@@ -425,10 +436,10 @@
                 stage(wa, u, u)
 
         when_unit(0, stage_q1)
+        when_unit(1, stage_p2)
+        when_unit(-1, stage_q2)
         pl.when(i == 2)(lambda: raw_landed(4))
         when_unit(2, stage_p1)
-        when_unit(1, stage_p2)
-        when_unit(-1, stage_q2)
         k = -1
         for section in range(4):
             for number, step in enumerate(READY[section]):
@@ -453,7 +464,8 @@
     done = jnp.int32(len(READY[0]))
     for section in range(1, 4):
         done = jnp.where(s == section, len(READY[section]), done)
-    pl.loop(done, 4)(forward)
+    pl.loop(done, 3)(forward)
+    forward_last()
 
     @pl.loop(0, 3 - s)
     def _(step):

time: 138 us -> 137 us (level)
  no operation moved by 1% of the time
where the time goes in v11:
time: 137 us
  Pallas kernels  136 us (99%)
  local copies, waits for them, and re-layouts  1.67 us (1%)
    pallas_call x1, Pallas kernels, local(): pl.pallas_call(kernel, out_shape=jax.ShapeDtypeStruct((32, D), F32), in_s...  136 us

profile of v11, /device:TPU:1, one launch (start us, length us, event | category | flops | bytes accessed | tf_op | source)
XLA Modules:
  0.0 137.2 jit_solution(7403682919661795414)
XLA Ops:
  0.0 135.5 %shard_map.46 = f32[32,2048]{1,0:T(8,128)} custom-call(bf16[4,64,2048]{2,1,0:T(8,128)(2,1)} %bitcast.5, bf16[32,2048]{1,0:T(8,128)(2,1)} %bitcast.7, bf16[256,2048]{1,0:T(8,128)(2,1)} %bitcast.6, s32[2,2]{1,0:T(2,128)} %len_ref.1), custom_call_target="tpu_custom_call" | custom-call | flops 19327352832 | bytes 37748736 | tf_op jit(solution)/shard_map/pallas_call | solution.py:727
  135.5 1.7 %copy.6 = f32[1,32,2048]{2,1,0:T(8,128)} copy(f32[1,32,2048]{2,1,0:T(8,128)} %bitcast.4) | data formatting | bytes 524288

commit v12 on v11

--- a/solution.py
+++ b/solution.py
@@ -467,14 +467,13 @@
     pl.loop(done, 3)(forward)
     forward_last()
 
-    @pl.loop(0, 3 - s)
-    def _(step):
+    def backward_step(step, order, after_first):
         k = 3 - step
         now = lax.rem(step + 1, 2)
         inv = iv[k][:, :1]
         factor = inv * inv * (jnp.sum(ms[...], axis=-1, keepdims=True) * (1.0 / D))
         sums = None
-        for j in range(2):
+        for j in order:
             tile = jnp.concatenate(
                 [
                     w[2 * k + h, j].reshape(HALF, width)
@@ -486,17 +485,22 @@
             g = lax.dot_general(
                 gp[now], tile, (((1,), (1,)), ((), ())), preferred_element_type=F32
             )
-            cols = pl.ds(j * HALF, HALF)
+            cols = part(j, 0, HALF)
             xf = xs[2 * k + j].reshape(ROWS, HALF).astype(F32)
             grad = (gr[:, cols].astype(F32) + inv * g - xf * factor).astype(BF16)
             gr[:, cols] = grad
             pre = (grad.astype(F32) * gd[k - 1, :, cols]).astype(BF16)
             gp[1 - now, :, cols] = pre
-            term = lane_sums(pre.astype(F32) * ub[k - 1, :, cols].astype(F32))
-            sums = term if sums is None else sums + term
-        ms[...] = sums
+            if after_first is None:
+                term = lane_sums(pre.astype(F32) * ub[k - 1, :, cols].astype(F32))
+                sums = term if sums is None else sums + term
+            elif j is order[0]:
+                after_first()
+        if sums is not None:
+            ms[...] = sums
 
     last_gp = lax.rem(s, 2)
+
     def column_part(core, hc):
         return part(core, hc * QUART, QUART)
 
@@ -506,8 +510,13 @@
             nsend.at[1 + hc], nrecv.at[1 + hc], sib,
         )
 
-    for hc in range(2):
-        give_g(hc).start()
+    def give():
+        for hc in range(2):
+            give_g(hc).start()
+
+    pl.loop(0, 2 - jnp.minimum(s, 2))(lambda step: backward_step(step, (0, 1), None))
+    pl.when(s < 3)(lambda: backward_step(2 - s, (1 - c, c), give))
+    pl.when(s == 3)(give)
     for hc in range(2):
         gw[c, :, CS[hc]] = gp[last_gp, :, column_part(c, hc)]
     remote(nw.at[1 - c], nw.at[1 - c], nsend.at[0], nrecv.at[0], sib).wait_recv()

time: 137 us -> 136 us (level)
  Pallas kernels: 136 us -> 134 us
    pallas_call x1, Pallas kernels: 136 us -> 134 us  [local(): pl.pallas_call(kernel, out_shape=jax.ShapeDtypeStruct((32, D), F32), in_s...]
where the time goes in v12:
time: 136 us
  Pallas kernels  134 us (99%)
  local copies, waits for them, and re-layouts  1.67 us (1%)
    pallas_call x1, Pallas kernels, local(): pl.pallas_call(kernel, out_shape=jax.ShapeDtypeStruct((32, D), F32), in_s...  134 us

profile of v12, /device:TPU:1, one launch (start us, length us, event | category | flops | bytes accessed | tf_op | source)
XLA Modules:
  0.0 135.6 jit_solution(6160038723291254448)
XLA Ops:
  0.0 134.0 %shard_map.46 = f32[32,2048]{1,0:T(8,128)} custom-call(bf16[4,64,2048]{2,1,0:T(8,128)(2,1)} %bitcast.5, bf16[32,2048]{1,0:T(8,128)(2,1)} %bitcast.7, bf16[256,2048]{1,0:T(8,128)(2,1)} %bitcast.6, s32[2,2]{1,0:T(2,128)} %len_ref.1), custom_call_target="tpu_custom_call" | custom-call | flops 19327352832 | bytes 37748736 | tf_op jit(solution)/shard_map/pallas_call | solution.py:736
  134.0 1.7 %copy.6 = f32[1,32,2048]{2,1,0:T(8,128)} copy(f32[1,32,2048]{2,1,0:T(8,128)} %bitcast.4) | data formatting | bytes 524288

commit v13 on v12

--- a/solution.py
+++ b/solution.py
@@ -406,13 +406,6 @@
     raw_step(2)
     stage_q1(wz, own, UNITS)
     stage_q1(wa, own, own)
-    for copy in in_x:
-        copy.wait()
-    for m in range(2):
-        for q in range(2):
-            rows = pl.ds(128 * m + 64 * q, 64)
-            live = lax.broadcasted_iota(jnp.int32, (64, D), 0) < lens[m, q]
-            gr[rows, :] = jnp.where(live, gr[rows, :].astype(F32), 0.0).astype(BF16)
     near = unit(1)
     stage_p1(wa, near, near)
     raw_step(3)
@@ -425,7 +418,6 @@
     raw_step(4)
     third = unit(2)
     stage_p1(wa, third, third)
-    norm(0)
 
     @pl.loop(1, UNITS + 2)
     def _(i):
@@ -446,6 +438,17 @@
                 k = jnp.where((s == section) & (i == step), number, k)
         pl.when(k >= 0)(lambda: forward(jnp.maximum(k, 0)))
         when_unit(-2, stage_f)
+        @pl.when(i == 1)
+        def _():
+            for copy in in_x:
+                copy.wait()
+            for m in range(2):
+                for q in range(2):
+                    rows = pl.ds(128 * m + 64 * q, 64)
+                    live = lax.broadcasted_iota(jnp.int32, (64, D), 0) < lens[m, q]
+                    gr[rows, :] = jnp.where(live, gr[rows, :].astype(F32), 0.0).astype(BF16)
+            norm(0)
+
         pl.when(i == 2)(lambda: relay(1, 0))
 
         @pl.when(i == 3)

time: 136 us -> 136 us (level)
  no operation moved by 1% of the time
where the time goes in v13:
time: 136 us; the launch traced here: 135 us
  Pallas kernels  134 us (99%)
  local copies, waits for them, and re-layouts  1.67 us (1%)
    pallas_call x1, Pallas kernels, local(): pl.pallas_call(kernel, out_shape=jax.ShapeDtypeStruct((32, D), F32), in_s...  134 us

profile of v13, /device:TPU:1, one launch (start us, length us, event | category | flops | bytes accessed | tf_op | source)
XLA Modules:
  0.0 135.5 jit_solution(15646636742456918820)
XLA Ops:
  0.0 133.8 %shard_map.46 = f32[32,2048]{1,0:T(8,128)} custom-call(bf16[4,64,2048]{2,1,0:T(8,128)(2,1)} %bitcast.5, bf16[32,2048]{1,0:T(8,128)(2,1)} %bitcast.7, bf16[256,2048]{1,0:T(8,128)(2,1)} %bitcast.6, s32[2,2]{1,0:T(2,128)} %len_ref.1), custom_call_target="tpu_custom_call" | custom-call | flops 19327352832 | bytes 37748736 | tf_op jit(solution)/shard_map/pallas_call | solution.py:739
  133.8 1.7 %copy.6 = f32[1,32,2048]{2,1,0:T(8,128)} copy(f32[1,32,2048]{2,1,0:T(8,128)} %bitcast.4) | data formatting | bytes 524288
